TPU v7x, 256 devices: a whole 4x4x8 slice. The times are simulated.
256 devices in a mesh: seq: 32 (over x, z), head: 8 (over y, core).
Axes of the slice: x: 4, y: 4, z: 8, core: 2. Of those that a mesh axis runs over, the one named last changes fastest.
Arguments:
- q_codes: bfloat16 [16384, 4096], P(('seq', 'head')), may hold values from -32 to 32
- q_exps: int32 [16384, 32], P(('seq', 'head')), may hold values from -1 to 1
- k_codes: bfloat16 [16384, 4096], P(('seq', 'head')), may hold values from -32 to 32
- k_exps: int32 [16384, 32], P(('seq', 'head')), may hold values from -1 to 1
- v_codes: bfloat16 [16384, 4096], P(('seq', 'head')), may hold values from -6 to 6
- v_exps: int32 [16384, 32], P(('seq', 'head')), may hold values from -1 to 1
- lin_query: bfloat16 [16384, 4096], P('seq', 'head'), may hold values from -6 to 6
- lin_keys: bfloat16 [16384, 4096], P('seq', 'head'), may hold values from -6 to 6
- lin_values: bfloat16 [16384, 4096], P('seq', 'head'), may hold values from -6 to 6
- decay_log: float32 [16384, 32], P('seq', 'head'), may hold values from -1 to 0
Outputs:
- soft_out: bfloat16 [16384, 4096], P(('seq', 'head'))
- lin_out: bfloat16 [16384, 4096], P('seq', 'head')
All inputs are finite; a program needn't handle non-finite values.
Results may differ from a plain program's by a relative error of at most 0.02.
Values may be sent and summed in bfloat16 or wider, within the bound.
No kernel may reach another device: no remote copies, remote signals or barrier semaphores. Data moves between devices by JAX's collectives and lax.ppermute only.
A program may use at most 192 MiB of HBM per device.

v0:
```python
import math

import jax
import jax.numpy as jnp
from jax import lax
from jax.experimental import pallas as pl
from jax.experimental.pallas import tpu as pltpu
from jax.sharding import PartitionSpec as P

STRETCH = 128
TILE = 256
HIDDEN = -1e30
VMEM = pl.BlockSpec(memory_space=pltpu.VMEM)
SMEM = pl.BlockSpec(memory_space=pltpu.SMEM)
ANY = pl.BlockSpec(memory_space=pl.ANY)
WHOLE = pl.BlockSpec()


def limits(megabytes):
    return pltpu.CompilerParams(vmem_limit_bytes=megabytes * 1024 * 1024)


def ring(value, steps):
    count = lax.axis_size("head")
    return lax.ppermute(value, "head", [(i, (i + steps) % count) for i in range(count)])


def core_swap(value):
    count = lax.axis_size("head")
    return lax.ppermute(value, "head", [(i, i ^ 1) for i in range(count)])


def after(value, *others):
    return lax.optimization_barrier((value, *others))[0]


def prepare(codes, exponents):
    heads, tokens = exponents[0].shape
    width = codes[0].shape[1] // heads
    count = len(codes)

    def kernel(*refs):
        out = refs[-1]
        for n in range(count):
            scale = jnp.exp2(refs[count + n][...].astype(jnp.float32)).T
            for h in range(heads):
                rows = refs[n][:, h * width : (h + 1) * width].astype(jnp.float32)
                rows = rows * scale[:, h : h + 1]
                out[h, n * tokens : (n + 1) * tokens, :] = rows.astype(jnp.bfloat16)

    return pl.pallas_call(
        kernel,
        in_specs=[WHOLE] * (2 * count),
        out_specs=VMEM,
        out_shape=jax.ShapeDtypeStruct((heads, count * tokens, width), jnp.bfloat16),
        compiler_params=limits(60),
    )(*codes, *exponents)


def attend(ranks, query, chunks, state, span, tail=None):
    seq_count, key_dev, head_dim = chunks[0].shape
    key_dev //= 2
    finish = tail is not None
    rows = seq_count * key_dev
    per = TILE // key_dev
    tiles = rows // TILE
    order = [*range(0, tiles, 2), *range(tiles - 1, 0, -2)]
    early = (max(order[:2]) + 1) * per
    chunk_count = len(chunks)
    pairs = chunk_count // 2
    scale = math.log2(math.e) / math.sqrt(head_dim)
    first = state is None

    def kernel(*refs):
        refs = list(refs)
        ranks_ref, q_ref = refs.pop(0), refs.pop(0)
        sources = [refs.pop(0) for _ in chunks]
        given = [] if first else [refs.pop(0) for _ in range(3)]
        tail_ref = refs.pop(0) if finish else None
        o_ref = refs.pop(0) if finish else None
        m_ref, l_ref, acc_ref, held, sems, score_a, score_b = refs
        score_refs = (score_a, score_b)
        parts = (slice(0, early), slice(early, seq_count))
        copies = [
            [
                pltpu.make_async_copy(sources[n].at[part], held.at[n, part], sems.at[n, m])
                for n in range(chunk_count)
            ]
            for m, part in enumerate(parts)
        ]
        for copy in copies[0] + copies[1]:
            copy.start()
        if finish:
            o_ref[:, key_dev:, :] = tail_ref[...]
        if first:
            m_ref[...] = jnp.full_like(m_ref, HIDDEN)
            l_ref[...] = jnp.zeros_like(l_ref)
            acc_ref[...] = jnp.zeros_like(acc_ref)
        else:
            m_ref[...] = given[0][...]
            l_ref[...] = given[1][...]
            acc_ref[...] = given[2][...]
        own = ranks_ref[0]

        def units(i):
            return [(c, j) for c in range(2) for j in range(i + 1)]

        def produce(p, slot, i, n, q, top):
            c, j = units(i)[n]
            keys = held[2 * p + c, j * per : (j + 1) * per, :key_dev, :].reshape(TILE, head_dim)
            s = lax.dot_general(
                keys, q, (((1,), (1,)), ((), ())), preferred_element_type=jnp.float32
            )
            if j == i:
                a = lax.broadcasted_iota(jnp.int32, (TILE, TILE), 0)
                b = lax.broadcasted_iota(jnp.int32, (TILE, TILE), 1)
                key_pos = a // key_dev * span + ranks_ref[1 + 2 * p + c] * key_dev + a % key_dev
                query_pos = b // key_dev * span + own * key_dev + b % key_dev
                s = jnp.where(key_pos <= query_pos, s, HIDDEN)
            score_refs[slot][n * TILE : (n + 1) * TILE, :] = s
            part = jnp.max(s.reshape(TILE // 8, 8, TILE), axis=0)
            return part if top is None else jnp.maximum(top, part)

        def consume(p, slot, i, n, offset, total, weighted):
            c, j = units(i)[n]
            s = score_refs[slot][n * TILE : (n + 1) * TILE, :]
            w = jnp.exp2(s * scale - offset)
            values = held[2 * p + c, j * per : (j + 1) * per, key_dev:, :].reshape(TILE, head_dim)
            x = lax.dot_general(
                values,
                w.astype(jnp.bfloat16),
                (((0,), (0,)), ((), ())),
                preferred_element_type=jnp.float32,
            )
            part = jnp.sum(w.reshape(TILE // 8, 8, TILE), axis=0)
            if total is None:
                return part, x
            return total + part, weighted + x

        def stage(p, at, before):
            i = order[at] if at < tiles else None
            done = order[at - 1] if at > 0 else None
            here, there = at % 2, (at + 1) % 2
            ahead = behind = 0
            if i is not None:
                q = q_ref[i * per : (i + 1) * per, :key_dev, :].reshape(TILE, head_dim)
                ahead = len(units(i))
            if done is not None:
                cols = slice(done * TILE, (done + 1) * TILE)
                old = m_ref[done : done + 1, :]
                new = jnp.maximum(old, jnp.max(before, axis=0, keepdims=True))
                m_ref[done : done + 1, :] = new
                fade = jnp.exp2((old - new) * scale)
                offset = new * scale
                behind = len(units(done))
            top = total = weighted = None
            a = b = 0
            while a < ahead or b < behind:
                if a < ahead and (b >= behind or a * behind <= b * ahead):
                    top = produce(p, here, i, a, q, top)
                    a += 1
                else:
                    total, weighted = consume(p, there, done, b, offset, total, weighted)
                    b += 1
            if done is not None:
                total = l_ref[done : done + 1, :] * fade + jnp.sum(total, axis=0, keepdims=True)
                weighted = acc_ref[:, cols] * fade + weighted
                if finish:
                    o = (weighted / total).T.astype(jnp.bfloat16).reshape(per, key_dev, head_dim)
                    o_ref[done * per : (done + 1) * per, :key_dev, :] = o
                else:
                    l_ref[done : done + 1, :] = total
                    acc_ref[:, cols] = weighted

            @pl.when(own < 0)
            def _():
                m_ref[0:1, :] = jnp.zeros((1, TILE), jnp.float32)

            return top

        def step(p, unused):
            def arrive(m):
                for n in range(chunk_count):

                    @pl.when(p == n // 2)
                    def _(n=n):
                        copies[m][n].wait()

            arrive(0)
            top = None
            for at in range(tiles + 1):
                if at == 2:
                    arrive(1)
                top = stage(p, at, top)
            return unused

        lax.fori_loop(0, pairs, step, 0)

    state_shape = [
        jax.ShapeDtypeStruct((tiles, TILE), jnp.float32),
        jax.ShapeDtypeStruct((tiles, TILE), jnp.float32),
        jax.ShapeDtypeStruct((head_dim, rows), jnp.float32),
    ]
    scratch = [
        pltpu.VMEM((chunk_count, seq_count, 2 * key_dev, head_dim), jnp.bfloat16),
        pltpu.SemaphoreType.DMA((chunk_count, 2)),
        pltpu.VMEM((2 * rows, TILE), jnp.float32),
        pltpu.VMEM((2 * rows, TILE), jnp.float32),
    ]
    if finish:
        out_rows = key_dev + tail.shape[1]
        out_shape = jax.ShapeDtypeStruct((seq_count, out_rows, head_dim), jnp.bfloat16)
        out_specs = VMEM
        scratch = [pltpu.VMEM(s.shape, s.dtype) for s in state_shape] + scratch
    else:
        out_shape, out_specs = state_shape, [VMEM] * 3
    extra = ([] if first else [*state]) + ([tail] if finish else [])
    flops = 2 * chunk_count * rows * rows * head_dim * 2
    return pl.pallas_call(
        kernel,
        in_specs=[SMEM, VMEM] + [ANY] * chunk_count + [VMEM] * len(extra),
        out_specs=out_specs,
        out_shape=out_shape,
        scratch_shapes=scratch,
        cost_estimate=pl.CostEstimate(
            flops=flops, bytes_accessed=(chunk_count + 2) * 2**20, transcendentals=flops // 1024
        ),
        compiler_params=limits(20),
    )(ranks, query, *chunks, *extra)


def summed(decay):
    tokens = decay.shape[1]
    a = lax.broadcasted_iota(jnp.int32, (tokens, tokens), 0)
    b = lax.broadcasted_iota(jnp.int32, (tokens, tokens), 1)
    ones = jnp.where(a <= b, 1.0, 0.0).astype(jnp.float32)
    cum = jnp.dot(
        decay, ones, precision=lax.Precision.HIGHEST, preferred_element_type=jnp.float32
    )
    return cum, cum.T


def prepare_rest(codes, exponents, query, keys, values, decay_rows, seq_count):
    soft_heads, tokens = exponents.shape
    width = codes.shape[1] // soft_heads
    rows = keys.shape[0]
    heads = decay_rows.shape[0]
    head_dim = keys.shape[1] // heads
    blocks = rows // STRETCH
    shares = seq_count // heads
    share = head_dim // shares

    def kernel(code_ref, exps_ref, q_ref, k_ref, v_ref, decay_ref, *out):
        packed_ref, inner_ref, decayed_ref, before_ref, fade_ref = out
        scale = jnp.exp2(exps_ref[...].astype(jnp.float32)).T
        for h in range(soft_heads):
            part = code_ref[:, h * width : (h + 1) * width].astype(jnp.float32)
            packed_ref[h, :tokens, :] = (part * scale[:, h : h + 1]).astype(jnp.bfloat16)
        a = lax.broadcasted_iota(jnp.int32, (STRETCH, STRETCH), 0)
        b = lax.broadcasted_iota(jnp.int32, (STRETCH, STRETCH), 1)
        causal = b <= a
        place = lax.broadcasted_iota(jnp.int32, (share, head_dim), 0)
        states = [jnp.zeros((head_dim, head_dim), jnp.float32)] * heads
        log_total = jnp.zeros((heads, 1), jnp.float32)
        for n in range(blocks):
            span = slice(n * STRETCH, (n + 1) * STRETCH)
            cum, cum_cols = summed(decay_ref[:, span])
            for h in range(heads):
                cols = slice(h * head_dim, (h + 1) * head_dim)
                q, k, v = q_ref[span, cols], k_ref[span, cols], v_ref[span, cols]
                here, end = cum_cols[:, h : h + 1], cum[h : h + 1, STRETCH - 1 : STRETCH]
                scores = lax.dot_general(
                    q, k, (((1,), (1,)), ((), ())), preferred_element_type=jnp.float32
                )
                gap = jnp.where(causal, here - cum[h : h + 1], 0.0)
                weights = jnp.where(causal, scores * jnp.exp(gap), 0.0).astype(jnp.bfloat16)
                inner_ref[span, cols] = jnp.dot(weights, v, preferred_element_type=jnp.float32)
                decayed = (q.astype(jnp.float32) * jnp.exp(here)).astype(jnp.bfloat16)
                decayed_ref[span, cols] = decayed
                before_ref[n, h] = states[h]
                fade = jnp.exp(log_total[h : h + 1])
                fade_ref[n * heads + h : n * heads + h + 1, :] = jnp.broadcast_to(
                    fade, (1, head_dim)
                )
                aged = (k.astype(jnp.float32) * jnp.exp(end - here)).astype(jnp.bfloat16)
                states[h] = jnp.exp(end) * states[h] + lax.dot_general(
                    aged, v, (((0,), (0,)), ((), ())), preferred_element_type=jnp.float32
                )
            log_total += cum[:, STRETCH - 1 : STRETCH]
        for h in range(heads):
            log = jnp.broadcast_to(log_total[h : h + 1], (share, head_dim))
            high = log.astype(jnp.bfloat16).astype(jnp.float32)
            mid = (log - high).astype(jnp.bfloat16).astype(jnp.float32)
            low = log - high - mid
            parts = jnp.where(place == 0, high, jnp.where(place == 1, mid, low))
            parts = jnp.where(place < 3, parts, 0.0).astype(jnp.bfloat16)
            state = states[h].astype(jnp.bfloat16)
            for n in range(shares):
                to = h * shares + n
                packed_ref[to, tokens : tokens + share, :] = state[n * share : (n + 1) * share]
                packed_ref[to, tokens + share :, :] = parts

    return pl.pallas_call(
        kernel,
        in_specs=[WHOLE] * 6,
        out_specs=[VMEM] * 5,
        out_shape=[
            jax.ShapeDtypeStruct((soft_heads, tokens + 2 * share, width), jnp.bfloat16),
            jax.ShapeDtypeStruct(keys.shape, jnp.float32),
            jax.ShapeDtypeStruct(keys.shape, jnp.bfloat16),
            jax.ShapeDtypeStruct((blocks, heads, head_dim, head_dim), jnp.float32),
            jax.ShapeDtypeStruct((blocks * heads, head_dim), jnp.float32),
        ],
        cost_estimate=pl.CostEstimate(
            flops=4 * 10**9, bytes_accessed=6 * 2**20, transcendentals=2**20
        ),
        compiler_params=limits(60),
    )(codes, exponents, query, keys, values, decay_rows)


def entering_states(arrived, tokens):
    seq_count, rows, head_dim = arrived.shape
    share = (rows - tokens) // 2

    def kernel(in_ref, out_ref):
        state = jnp.zeros((share, head_dim), jnp.float32)
        for s in range(seq_count):
            out_ref[s] = state.astype(jnp.bfloat16)
            parts = in_ref[s, tokens + share :, :].astype(jnp.float32)
            fade = jnp.exp(jnp.sum(parts, axis=0, keepdims=True))
            state = fade * state + in_ref[s, tokens : tokens + share, :].astype(jnp.float32)

    return pl.pallas_call(
        kernel,
        in_specs=[VMEM],
        out_specs=VMEM,
        out_shape=jax.ShapeDtypeStruct((seq_count, share, head_dim), jnp.bfloat16),
        compiler_params=limits(8),
    )(arrived)


def finish(returned, tokens, inner, decayed, before, fades):
    soft_heads, rows, width = returned.shape
    blocks, heads, head_dim, _ = before.shape
    shares = soft_heads // heads
    share = rows - tokens

    def kernel(in_ref, inner_ref, decayed_ref, before_ref, fade_ref, soft_ref, lin_ref):
        for h in range(soft_heads):
            soft_ref[:, h * width : (h + 1) * width] = in_ref[h, :tokens, :]
        for h in range(heads):
            cols = slice(h * head_dim, (h + 1) * head_dim)
            entering = in_ref[h * shares : (h + 1) * shares, tokens:, :].astype(jnp.float32)
            entering = entering.reshape(head_dim, head_dim)
            for n in range(blocks):
                span = slice(n * STRETCH, (n + 1) * STRETCH)
                fade = fade_ref[n * heads + h : n * heads + h + 1, :]
                state = (fade * entering + before_ref[n, h]).astype(jnp.bfloat16)
                mixed = inner_ref[span, cols] + jnp.dot(
                    decayed_ref[span, cols], state, preferred_element_type=jnp.float32
                )
                mean = jnp.mean(mixed * mixed, axis=1, keepdims=True)
                lin_ref[span, cols] = (mixed / jnp.sqrt(mean + 1e-06)).astype(jnp.bfloat16)

    return pl.pallas_call(
        kernel,
        in_specs=[VMEM] * 5,
        out_specs=[VMEM] * 2,
        out_shape=[
            jax.ShapeDtypeStruct((tokens, soft_heads * width), jnp.bfloat16),
            jax.ShapeDtypeStruct(inner.shape, jnp.bfloat16),
        ],
        compiler_params=limits(16),
    )(returned, inner, decayed, before, fades)


def shards(
    q_codes, q_exps, k_codes, k_exps, v_codes, v_exps, lin_query, lin_keys, lin_values, decay_log
):
    rank = lax.axis_index("head")
    count = lax.axis_size("head")
    seq_count = lax.axis_size("seq")
    tokens = q_codes.shape[0]
    span = tokens * count

    def ranks(*steps):
        chip, core = rank // 2, rank % 2
        listed = [rank]
        for chips, cores in steps:
            listed.append((chip + chips) % (count // 2) * 2 + (core + cores) % 2)
        return jnp.stack(listed).astype(jnp.int32)

    def exchange(value):
        return lax.all_to_all(value, "seq", split_axis=0, concat_axis=0, tiled=True)

    packed = prepare((k_codes, v_codes), (k_exps.T, v_exps.T))
    own = exchange(packed)
    lin = after((lin_query, lin_keys, lin_values, decay_log.T), packed)
    packed, inner, decayed, before, fades = prepare_rest(q_codes, q_exps.T, *lin, seq_count)
    arrived = exchange(packed)
    own = after(own, packed)
    below = ring(own, 2)
    above = ring(own, -2)
    partner = core_swap(own)
    arrived = after(arrived, below, above)
    outward = jnp.where(rank % 2 == 0, below, above)
    far = lax.ppermute(
        outward, "head", [(i, (i + 2 - i % 2 * 4) % count) for i in range(count)]
    )
    below_other = core_swap(below)
    above_other = core_swap(above)
    state = attend(ranks((0, 0), (0, 1)), arrived, [own, partner], None, span)
    entering = entering_states(arrived, tokens)
    far_other = core_swap(after(far, state[0]))
    state = attend(
        ranks((-1, 0), (-1, 1), (1, 0), (1, 1)),
        arrived,
        [below, below_other, above, above_other],
        state,
        span,
    )
    attended = attend(
        ranks((2, 0), (2, 1)), arrived, [far, far_other], state, span, tail=entering
    )
    returned = exchange(attended)
    return tuple(finish(returned, tokens, inner, decayed, before, fades))


def solution(mesh):
    rows = P(("seq", "head"), None)
    tiles = P("seq", "head")
    return jax.shard_map(
        shards,
        mesh=mesh,
        in_specs=(rows,) * 6 + (tiles,) * 4,
        out_specs=(rows, tiles),
        check_vma=False,
    )
```

profile of v0, /device:TPU:32, one launch (start us, length us, event | category | flops | bytes accessed | tf_op | source)
XLA Modules:
  0.0 138.3 jit_solution(7405720973567530392)
XLA Ops:
  0.6 3.0 %shard_map.113 = bf16[32,128,128]{2,1,0:T(8,128)(2,1)} custom-call(bf16[64,4096]{1,0:T(8,128)(2,1)} %refs_0_.1, bf16[64,4096]{1,0:T(8,128)(2,1)} %refs_1_.1, s32[32,64]{1,0:T(8,128)} %bitcast.13, s32[32,64]{1,0:T(8,128)} %bitcast.14), custom_call_target="tpu_custom_call" | custom-call | tf_op jit(solution)/shard_map/pallas_call | solution.py:51
  3.6 11.2 %all-to-all-start.1 = ((bf16[32,128,128]{2,1,0:T(8,128)(2,1)}), bf16[32,128,128]{2,1,0:T(8,128)(2,1)}, u32[]{:S(2)}, u32[]{:S(2)}) async-start(bf16[32,128,128]{2,1,0:T(8,128)(2,1)} %shard_map.113), calls=%async_computation.1 | async-start | bytes 2097152 | tf_op jit(solution)/shard_map/all_to_all | solution.py:394
  14.9 6.6 %shard_map.114 = (bf16[32,96,128]{2,1,0:T(8,128)(2,1)}, f32[512,512]{1,0:T(8,128)}, bf16[512,512]{1,0:T(8,128)(2,1)}, f32[4,4,128,128]{3,2,1,0:T(8,128)}, f32[16,128]{1,0:T(8,128)}) custom-call(bf16[64,4096]{1,0:T(8,128)(2,1)} %code_ref.1, s32[32,64]{1,0:T(8,128)} %bitcast.15, bf16[512,512]{1,0:T(8,128)(2,1)} %q_ref, bf16[512,512]{1,0:T(8,128)(2,1)} %k_ref, ...), custom_call_target="tpu_custom_call" | custom-call | flops 4000000000 | bytes 6291456 | tf_op jit(solution)/shard_map/pallas_call | solution.py:303
  21.5 22.0 %all-to-all-done.1.refs_2_ = bf16[32,128,128]{2,1,0:T(8,128)(2,1)} async-done(((bf16[32,128,128]{2,1,0:T(8,128)(2,1)}), bf16[32,128,128]{2,1,0:T(8,128)(2,1)}, u32[]{:S(2)}, u32[]{:S(2)}) %all-to-all-start.1) | async-done | bytes 1048608 | tf_op jit(solution)/shard_map/all_to_all | solution.py:394
  43.5 1.6 %collective-permute-start = (bf16[32,128,128]{2,1,0:T(8,128)(2,1)}, bf16[32,128,128]{2,1,0:T(8,128)(2,1)S(1)}, u32[]{:S(2)}, u32[]{:S(2)}) collective-permute-start(bf16[32,128,128]{2,1,0:T(8,128)(2,1)} %all-to-all-done.1.refs_2_), channel_id=1, source_target_pairs={{0,2},{1,3},{2,4},{3,5},{4,6},{5,7},{6,0},{7,1},{8,10},{9,11},{10,... | collective-permute-start | bytes 3145736 | tf_op jit(solution)/shard_map/ppermute | solution.py:25
  45.0 1.7 %collective-permute-start.1 = (bf16[32,128,128]{2,1,0:T(8,128)(2,1)}, bf16[32,128,128]{2,1,0:T(8,128)(2,1)S(1)}, u32[]{:S(2)}, u32[]{:S(2)}) collective-permute-start(bf16[32,128,128]{2,1,0:T(8,128)(2,1)} %all-to-all-done.1.refs_2_), channel_id=1, source_target_pairs={{0,6},{1,7},{2,0},{3,1},{4,2},{5,3},{6,4},{7,5},{8,14},{9,15},{10,... | collective-permute-start | bytes 3145736 | tf_op jit(solution)/shard_map/ppermute | solution.py:25
  46.7 5.2 %all-to-all-start = ((bf16[32,96,128]{2,1,0:T(8,128)(2,1)}), bf16[32,96,128]{2,1,0:T(8,128)(2,1)S(1)}, u32[]{:S(2)}, u32[]{:S(2)}) async-start(bf16[32,96,128]{2,1,0:T(8,128)(2,1)} %get-tuple-element.24), calls=%async_computation | async-start | bytes 1572864 | tf_op jit(solution)/shard_map/all_to_all | solution.py:394
  51.9 0.1 collective-permute-start.3
  52.0 15.7 %collective-permute-done.refs_2_ = bf16[32,128,128]{2,1,0:T(8,128)(2,1)S(1)} collective-permute-done((bf16[32,128,128]{2,1,0:T(8,128)(2,1)}, bf16[32,128,128]{2,1,0:T(8,128)(2,1)S(1)}, u32[]{:S(2)}, u32[]{:S(2)}) %collective-permute-start) | collective-permute-done | bytes 1048608 | tf_op jit(solution)/shard_map/ppermute | solution.py:25
  67.7 0.0 collective-permute-done.1.refs_4_
  67.7 1.2 broadcast_select_fusion
  68.9 1.6 %collective-permute-start.2 = (bf16[32,128,128]{2,1,0:T(8,128)(2,1)}, bf16[32,128,128]{2,1,0:T(8,128)(2,1)}, u32[]{:S(2)}, u32[]{:S(2)}) collective-permute-start(bf16[32,128,128]{2,1,0:T(8,128)(2,1)} %broadcast_select_fusion), channel_id=1, source_target_pairs={{0,2},{1,7},{2,4},{3,1},{4,6},{5,3},{6,0},{7,5},{8,10},{9,15},{10,... | collective-permute-start | bytes 3145736 | tf_op jit(solution)/shard_map/ppermute | solution.py:407
  70.4 0.0 collective-permute-start.5
  70.4 0.5 collective-permute-start.6
  70.9 0.1 pad_add_fusion.1.refs_0_
  71.0 3.0 %all-to-all-done.refs_1_.in_ref = bf16[32,96,128]{2,1,0:T(8,128)(2,1)S(1)} async-done(((bf16[32,96,128]{2,1,0:T(8,128)(2,1)}), bf16[32,96,128]{2,1,0:T(8,128)(2,1)S(1)}, u32[]{:S(2)}, u32[]{:S(2)}) %all-to-all-start) | async-done | bytes 786464 | tf_op jit(solution)/shard_map/all_to_all | solution.py:394
  74.1 0.0 collective-permute-done.3.refs_3_
  74.1 7.8 %shard_map.115 = (f32[8,256]{1,0:T(8,128)S(1)}, f32[8,256]{1,0:T(8,128)S(1)}, f32[128,2048]{1,0:T(8,128)S(1)}) custom-call(s32[3]{0:T(128)S(1)} %pad_add_fusion.1.refs_0_, bf16[32,96,128]{2,1,0:T(8,128)(2,1)S(1)} %all-to-all-done.refs_1_.in_ref, bf16[32,128,128]{2,1,0:T(8,128)(2,1)} %all-to-all-done.1.refs_2_, ...), custom_call_target="tpu_custom_call" | custom-call | flops 4294967296 | bytes 4194304 | tf_op jit(solution)/shard_map/pallas_call | solution.py:219
  81.9 0.0 copy-start.4
  81.9 1.0 copy-done.4
  82.8 2.3 %collective-permute-done.2.refs_2_ = bf16[32,128,128]{2,1,0:T(8,128)(2,1)} collective-permute-done((bf16[32,128,128]{2,1,0:T(8,128)(2,1)}, bf16[32,128,128]{2,1,0:T(8,128)(2,1)}, u32[]{:S(2)}, u32[]{:S(2)}) %collective-permute-start.2) | collective-permute-done | bytes 1048608 | tf_op jit(solution)/shard_map/ppermute | solution.py:407
  85.2 0.0 collective-permute-start.4
  85.2 0.1 stack.49.refs_0_
  85.3 0.1 pad_add_fusion.refs_0_
  85.3 0.1 shard_map.117.refs_7_
  85.4 0.0 collective-permute-done.5.refs_3_
  85.4 0.0 collective-permute-done.6.refs_5_
  85.5 0.0 copy-start.5
  85.5 1.2 copy-done.5
  86.7 13.7 %shard_map.116 = (f32[8,256]{1,0:T(8,128)S(1)}, f32[8,256]{1,0:T(8,128)S(1)}, f32[128,2048]{1,0:T(8,128)S(1)}) custom-call(s32[5]{0:T(128)S(1)} %stack.49.refs_0_, bf16[32,96,128]{2,1,0:T(8,128)(2,1)S(1)} %all-to-all-done.refs_1_.in_ref, bf16[32,128,128]{2,1,0:T(8,128)(2,1)S(1)} %collective-permute-done.refs_2_, ...), custom_call_target="tpu_custom_call" | custom-call | flops 8589934592 | bytes 6291456 | tf_op jit(solution)/shard_map/pallas_call | solution.py:219
  100.4 0.0 collective-permute-done.4.refs_3_
  100.4 0.0 copy-start.1
  100.4 0.0 copy-start.2
  100.4 8.3 %shard_map.118 = bf16[32,80,128]{2,1,0:T(8,128)(2,1)S(1)} custom-call(s32[3]{0:T(128)S(1)} %pad_add_fusion.refs_0_, bf16[32,96,128]{2,1,0:T(8,128)(2,1)S(1)} %all-to-all-done.refs_1_.in_ref, bf16[32,128,128]{2,1,0:T(8,128)(2,1)} %collective-permute-done.2.refs_2_, bf16[32,128,128]{2,1,0:T(8,128)(2,1)} %collective-permute-done.4.refs_3_, ...), custom_call_target="tpu_custom_call" | custom-call | flops 4294967296 | bytes 4194304 | tf_op jit(solution)/shard_map/pallas_call | solution.py:219
  108.7 0.0 copy-start
  108.7 0.0 copy-start.3
  108.7 27.8 %all_to_all.15.in_ref = bf16[32,80,128]{2,1,0:T(8,128)(2,1)S(1)} all-to-all(bf16[32,80,128]{2,1,0:T(8,128)(2,1)S(1)} %shard_map.118), channel_id=1, replica_groups=mesh['seq'=32,'head'=8] {'seq'}, dimensions={0} | all-to-all | bytes 1310720 | tf_op jit(solution)/shard_map/all_to_all | solution.py:394
  136.5 0.0 copy-done.1
  136.5 0.0 copy-done.2
  136.5 0.0 copy-done
  136.5 0.0 copy-done.3
  136.5 1.7 %shard_map.119 = (bf16[64,4096]{1,0:T(8,128)(2,1)}, bf16[512,512]{1,0:T(8,128)(2,1)}) custom-call(bf16[32,80,128]{2,1,0:T(8,128)(2,1)S(1)} %all_to_all.15.in_ref, f32[512,512]{1,0:T(8,128)S(1)} %copy-done, bf16[512,512]{1,0:T(8,128)(2,1)S(1)} %copy-done.2, f32[4,4,128,128]{3,2,1,0:T(8,128)S(1)} %copy-done.1, f32[16,128]{1,0:T(8,128)S(1)} %copy-done.3), custom_call_target="tpu_custom_call" | custom-call | tf_op jit(solution)/shard_map/pallas_call | solution.py:365
Async XLA Ops:
  3.6 39.8 %all-to-all-start.1 = ((bf16[32,128,128]{2,1,0:T(8,128)(2,1)}), bf16[32,128,128]{2,1,0:T(8,128)(2,1)}, u32[]{:S(2)}, u32[]{:S(2)}) async-start(bf16[32,128,128]{2,1,0:T(8,128)(2,1)} %shard_map.113), calls=%async_computation.1 | async-start | bytes 2097152 | tf_op jit(solution)/shard_map/all_to_all | solution.py:394
  43.5 24.2 %collective-permute-start = (bf16[32,128,128]{2,1,0:T(8,128)(2,1)}, bf16[32,128,128]{2,1,0:T(8,128)(2,1)S(1)}, u32[]{:S(2)}, u32[]{:S(2)}) collective-permute-start(bf16[32,128,128]{2,1,0:T(8,128)(2,1)} %all-to-all-done.1.refs_2_), channel_id=1, source_target_pairs={{0,2},{1,3},{2,4},{3,5},{4,6},{5,7},{6,0},{7,1},{8,10},{9,11},{10,... | collective-permute-start | bytes 3145736 | tf_op jit(solution)/shard_map/ppermute | solution.py:25
  45.0 22.7 %collective-permute-start.1 = (bf16[32,128,128]{2,1,0:T(8,128)(2,1)}, bf16[32,128,128]{2,1,0:T(8,128)(2,1)S(1)}, u32[]{:S(2)}, u32[]{:S(2)}) collective-permute-start(bf16[32,128,128]{2,1,0:T(8,128)(2,1)} %all-to-all-done.1.refs_2_), channel_id=1, source_target_pairs={{0,6},{1,7},{2,0},{3,1},{4,2},{5,3},{6,4},{7,5},{8,14},{9,15},{10,... | collective-permute-start | bytes 3145736 | tf_op jit(solution)/shard_map/ppermute | solution.py:25
  46.7 27.4 %all-to-all-start = ((bf16[32,96,128]{2,1,0:T(8,128)(2,1)}), bf16[32,96,128]{2,1,0:T(8,128)(2,1)S(1)}, u32[]{:S(2)}, u32[]{:S(2)}) async-start(bf16[32,96,128]{2,1,0:T(8,128)(2,1)} %get-tuple-element.24), calls=%async_computation | async-start | bytes 1572864 | tf_op jit(solution)/shard_map/all_to_all | solution.py:394
  51.9 22.2 %collective-permute-start.3 = (bf16[32,128,128]{2,1,0:T(8,128)(2,1)}, bf16[32,128,128]{2,1,0:T(8,128)(2,1)}, u32[]{:S(2)}, u32[]{:S(2)}) collective-permute-start(bf16[32,128,128]{2,1,0:T(8,128)(2,1)} %all-to-all-done.1.refs_2_), channel_id=1, source_target_pairs={{0,1},{1,0},{2,3},{3,2},{4,5},{5,4},{6,7},{7,6},{8,9},{9,8},{10,11... | collective-permute-start | bytes 3145736 | tf_op jit(solution)/shard_map/ppermute | solution.py:30
  68.9 16.3 %collective-permute-start.2 = (bf16[32,128,128]{2,1,0:T(8,128)(2,1)}, bf16[32,128,128]{2,1,0:T(8,128)(2,1)}, u32[]{:S(2)}, u32[]{:S(2)}) collective-permute-start(bf16[32,128,128]{2,1,0:T(8,128)(2,1)} %broadcast_select_fusion), channel_id=1, source_target_pairs={{0,2},{1,7},{2,4},{3,1},{4,6},{5,3},{6,0},{7,5},{8,10},{9,15},{10,... | collective-permute-start | bytes 3145736 | tf_op jit(solution)/shard_map/ppermute | solution.py:407
  70.4 15.0 %collective-permute-start.5 = (bf16[32,128,128]{2,1,0:T(8,128)(2,1)S(1)}, bf16[32,128,128]{2,1,0:T(8,128)(2,1)}, u32[]{:S(2)}, u32[]{:S(2)}) collective-permute-start(bf16[32,128,128]{2,1,0:T(8,128)(2,1)S(1)} %collective-permute-done.refs_2_), channel_id=1, source_target_pairs={{0,1},{1,0},{2,3},{3,2},{4,5},{5,4},{6,7},{7,6},{8,9},{9,8},{10,11... | collective-permute-start | bytes 3145736 | tf_op jit(solution)/shard_map/ppermute | solution.py:30
  70.4 15.0 %collective-permute-start.6 = (bf16[32,128,128]{2,1,0:T(8,128)(2,1)S(1)}, bf16[32,128,128]{2,1,0:T(8,128)(2,1)}, u32[]{:S(2)}, u32[]{:S(2)}) collective-permute-start(bf16[32,128,128]{2,1,0:T(8,128)(2,1)S(1)} %collective-permute-done.1.refs_4_), channel_id=1, source_target_pairs={{0,1},{1,0},{2,3},{3,2},{4,5},{5,4},{6,7},{7,6},{8,9},{9,8},{10,11... | collective-permute-start | bytes 3145736 | tf_op jit(solution)/shard_map/ppermute | solution.py:30
  81.9 1.0 copy-start.4
  85.2 15.2 %collective-permute-start.4 = (bf16[32,128,128]{2,1,0:T(8,128)(2,1)}, bf16[32,128,128]{2,1,0:T(8,128)(2,1)}, u32[]{:S(2)}, u32[]{:S(2)}) collective-permute-start(bf16[32,128,128]{2,1,0:T(8,128)(2,1)} %collective-permute-done.2.refs_2_), channel_id=1, source_target_pairs={{0,1},{1,0},{2,3},{3,2},{4,5},{5,4},{6,7},{7,6},{8,9},{9,8},{10,11... | collective-permute-start | bytes 3145736 | tf_op jit(solution)/shard_map/ppermute | solution.py:30
  85.5 1.2 copy-start.5
  100.4 36.1 %copy-start.1 = (f32[4,4,128,128]{3,2,1,0:T(8,128)S(1)}, f32[4,4,128,128]{3,2,1,0:T(8,128)}, u32[]{:S(2)}) copy-start(f32[4,4,128,128]{3,2,1,0:T(8,128)} %get-tuple-element.36.before_ref) | copy-start | bytes 3145732
  100.4 36.1 %copy-start.2 = (bf16[512,512]{1,0:T(8,128)(2,1)S(1)}, bf16[512,512]{1,0:T(8,128)(2,1)}, u32[]{:S(2)}) copy-start(bf16[512,512]{1,0:T(8,128)(2,1)} %get-tuple-element.35.decayed_ref) | copy-start | bytes 1572868
  108.7 27.9 %copy-start = (f32[512,512]{1,0:T(8,128)S(1)}, f32[512,512]{1,0:T(8,128)}, u32[]{:S(2)}) copy-start(f32[512,512]{1,0:T(8,128)} %get-tuple-element.34.inner_ref) | copy-start | bytes 3145732
  108.7 27.9 %copy-start.3 = (f32[16,128]{1,0:T(8,128)S(1)}, f32[16,128]{1,0:T(8,128)}, u32[]{:S(2)}) copy-start(f32[16,128]{1,0:T(8,128)} %get-tuple-element.37.fade_ref) | copy-start | bytes 24580
where the time goes:
time: 139 us; the launch traced here: 138 us
  waiting for transfers between devices  43 us (31%)
  Pallas kernels  41.2 us (30%)
  blocking collectives  27.8 us (20%)
  starting transfers between devices  21.8 us (16%)
  local copies, waits for them, and re-layouts  2.29 us (2%)
    pallas_call x3, Pallas kernels, attend(): pl.pallas_call(kernel, in_specs=[SMEM, VMEM] + [ANY] * chunk_count + [VME...  29.7 us
    all_to_all x1, blocking collectives, exchange(): return lax.all_to_all(value, 'seq', split_axis=0, concat_axis=0, tiled=True)  27.8 us
    all_to_all x2, waiting for transfers between devices, exchange(): return lax.all_to_all(value, 'seq', split_axis=0, concat_axis=0, tiled=True)  25 us
    all_to_all x2, starting transfers between devices, exchange(): return lax.all_to_all(value, 'seq', split_axis=0, concat_axis=0, tiled=True)  16.4 us
    ppermute x2, waiting for transfers between devices, ring(): lax.ppermute(value, 'head', [(i, (i + steps) % count) for i in range(coun...  15.7 us
    pallas_call x1, Pallas kernels, prepare_rest(): pl.pallas_call(kernel, in_specs=[WHOLE] * 6, out_specs=[VMEM] * 5, out_sh...  6.61 us
    ppermute x2, starting transfers between devices, ring(): lax.ppermute(value, 'head', [(i, (i + steps) % count) for i in range(coun...  3.24 us
    pallas_call x1, Pallas kernels, prepare(): pl.pallas_call(kernel, in_specs=[WHOLE] * (2 * count), out_specs=VMEM, ou...  3.01 us
  transfers between devices with their start and end apart: 9, of which 4 were waited for; matrix products, arithmetic and copies ran while one was open for 1% of the time, Pallas kernels for 20%

commit v1 on v0

--- a/solution.py
+++ b/solution.py
@@ -8,7 +8,8 @@
 from jax.sharding import PartitionSpec as P
 
 STRETCH = 128
-TILE = 256
+TILE = 512
+KEYS = 256
 HIDDEN = -1e30
 VMEM = pl.BlockSpec(memory_space=pltpu.VMEM)
 SMEM = pl.BlockSpec(memory_space=pltpu.SMEM)
@@ -20,11 +21,6 @@
     return pltpu.CompilerParams(vmem_limit_bytes=megabytes * 1024 * 1024)
 
 
-def ring(value, steps):
-    count = lax.axis_size("head")
-    return lax.ppermute(value, "head", [(i, (i + steps) % count) for i in range(count)])
-
-
 def core_swap(value):
     count = lax.axis_size("head")
     return lax.ppermute(value, "head", [(i, i ^ 1) for i in range(count)])
@@ -41,11 +37,13 @@
 
     def kernel(*refs):
         out = refs[-1]
+        row = lax.broadcasted_iota(jnp.int32, (heads, width), 0)
         for n in range(count):
-            scale = jnp.exp2(refs[count + n][...].astype(jnp.float32)).T
+            scale = jnp.exp2(refs[count + n][...].astype(jnp.float32)).T.astype(jnp.bfloat16)
             for h in range(heads):
-                rows = refs[n][:, h * width : (h + 1) * width].astype(jnp.float32)
-                rows = rows * scale[:, h : h + 1]
+                pick = jnp.where(row == h, 1.0, 0.0).astype(jnp.bfloat16)
+                wide = jnp.dot(scale, pick, preferred_element_type=jnp.float32)
+                rows = refs[n][:, h * width : (h + 1) * width].astype(jnp.float32) * wide
                 out[h, n * tokens : (n + 1) * tokens, :] = rows.astype(jnp.bfloat16)
 
     return pl.pallas_call(
@@ -65,7 +63,7 @@
     per = TILE // key_dev
     tiles = rows // TILE
     order = [*range(0, tiles, 2), *range(tiles - 1, 0, -2)]
-    early = (max(order[:2]) + 1) * per
+    early = (order[0] + 1) * per
     chunk_count = len(chunks)
     pairs = chunk_count // 2
     scale = math.log2(math.e) / math.sqrt(head_dim)
@@ -103,42 +101,58 @@
         own = ranks_ref[0]
 
         def units(i):
-            return [(c, j) for c in range(2) for j in range(i + 1)]
+            return [(c, j) for c in range(2) for j in range((i + 1) * TILE // KEYS)]
+
+        def first_column(i, j):
+            return max(0, j * KEYS - i * TILE)
+
+        def joined(old, new, start, how):
+            if old is None:
+                return new
+            if start == 0:
+                return how(old, new)
+            return jnp.concatenate([old[:, :start], how(old[:, start:], new)], axis=1)
 
         def produce(p, slot, i, n, q, top):
             c, j = units(i)[n]
-            keys = held[2 * p + c, j * per : (j + 1) * per, :key_dev, :].reshape(TILE, head_dim)
+            start = first_column(i, j)
+            blocks = slice(j * KEYS // key_dev, (j + 1) * KEYS // key_dev)
+            keys = held[2 * p + c, blocks, :key_dev, :].reshape(KEYS, head_dim)
             s = lax.dot_general(
-                keys, q, (((1,), (1,)), ((), ())), preferred_element_type=jnp.float32
+                keys, q[start:], (((1,), (1,)), ((), ())), preferred_element_type=jnp.float32
             )
-            if j == i:
-                a = lax.broadcasted_iota(jnp.int32, (TILE, TILE), 0)
-                b = lax.broadcasted_iota(jnp.int32, (TILE, TILE), 1)
+            if j * KEYS >= i * TILE:
+                a = lax.broadcasted_iota(jnp.int32, (KEYS, KEYS), 0)
+                b = lax.broadcasted_iota(jnp.int32, (KEYS, KEYS), 1)
                 key_pos = a // key_dev * span + ranks_ref[1 + 2 * p + c] * key_dev + a % key_dev
                 query_pos = b // key_dev * span + own * key_dev + b % key_dev
-                s = jnp.where(key_pos <= query_pos, s, HIDDEN)
-            score_refs[slot][n * TILE : (n + 1) * TILE, :] = s
-            part = jnp.max(s.reshape(TILE // 8, 8, TILE), axis=0)
-            return part if top is None else jnp.maximum(top, part)
+                corner = jnp.where(key_pos <= query_pos, s[:, :KEYS], HIDDEN)
+                if s.shape[1] > KEYS:
+                    corner = jnp.concatenate([corner, s[:, KEYS:]], axis=1)
+                s = corner
+            score_refs[slot][n * KEYS : (n + 1) * KEYS, start:] = s
+            part = jnp.max(s.reshape(KEYS // 8, 8, TILE - start), axis=0)
+            return joined(top, part, start, jnp.maximum)
 
         def consume(p, slot, i, n, offset, total, weighted):
             c, j = units(i)[n]
-            s = score_refs[slot][n * TILE : (n + 1) * TILE, :]
-            w = jnp.exp2(s * scale - offset)
-            values = held[2 * p + c, j * per : (j + 1) * per, key_dev:, :].reshape(TILE, head_dim)
+            start = first_column(i, j)
+            s = score_refs[slot][n * KEYS : (n + 1) * KEYS, start:]
+            w = jnp.exp2(s * scale - offset[:, start:])
+            blocks = slice(j * KEYS // key_dev, (j + 1) * KEYS // key_dev)
+            values = held[2 * p + c, blocks, key_dev:, :].reshape(KEYS, head_dim)
             x = lax.dot_general(
                 values,
                 w.astype(jnp.bfloat16),
                 (((0,), (0,)), ((), ())),
                 preferred_element_type=jnp.float32,
             )
-            part = jnp.sum(w.reshape(TILE // 8, 8, TILE), axis=0)
-            if total is None:
-                return part, x
-            return total + part, weighted + x
+            part = jnp.sum(w.reshape(KEYS // 8, 8, TILE - start), axis=0)
+            return joined(total, part, start, jnp.add), joined(weighted, x, start, jnp.add)
 
         def stage(p, at, before):
-            i = order[at] if at < tiles else None
+            i = order[at % tiles] if at < tiles or pairs > 1 else None
+            source = p if at < tiles else jnp.minimum(p + 1, pairs - 1)
             done = order[at - 1] if at > 0 else None
             here, there = at % 2, (at + 1) % 2
             ahead = behind = 0
@@ -157,7 +171,7 @@
             a = b = 0
             while a < ahead or b < behind:
                 if a < ahead and (b >= behind or a * behind <= b * ahead):
-                    top = produce(p, here, i, a, q, top)
+                    top = produce(source, here, i, a, q, top)
                     a += 1
                 else:
                     total, weighted = consume(p, there, done, b, offset, total, weighted)
@@ -178,23 +192,28 @@
 
             return top
 
-        def step(p, unused):
-            def arrive(m):
-                for n in range(chunk_count):
-
-                    @pl.when(p == n // 2)
-                    def _(n=n):
-                        copies[m][n].wait()
-
-            arrive(0)
-            top = None
-            for at in range(tiles + 1):
-                if at == 2:
-                    arrive(1)
+        def arrive(p, m):
+            for n in range(chunk_count):
+
+                @pl.when(p == n // 2)
+                def _(n=n):
+                    copies[m][n].wait()
+
+        def step(p, top):
+            for at in range(1, tiles + 1):
+                if at == 1:
+                    arrive(p, 1)
+                if at == tiles:
+                    arrive(p + 1, 0)
                 top = stage(p, at, top)
-            return unused
-
-        lax.fori_loop(0, pairs, step, 0)
+            return top
+
+        arrive(0, 0)
+        top = stage(0, 0, None)
+        if pairs > 1:
+            lax.fori_loop(0, pairs, step, top)
+        else:
+            step(0, top)
 
     state_shape = [
         jax.ShapeDtypeStruct((tiles, TILE), jnp.float32),
@@ -215,17 +234,13 @@
     else:
         out_shape, out_specs = state_shape, [VMEM] * 3
     extra = ([] if first else [*state]) + ([tail] if finish else [])
-    flops = 2 * chunk_count * rows * rows * head_dim * 2
     return pl.pallas_call(
         kernel,
         in_specs=[SMEM, VMEM] + [ANY] * chunk_count + [VMEM] * len(extra),
         out_specs=out_specs,
         out_shape=out_shape,
         scratch_shapes=scratch,
-        cost_estimate=pl.CostEstimate(
-            flops=flops, bytes_accessed=(chunk_count + 2) * 2**20, transcendentals=flops // 1024
-        ),
-        compiler_params=limits(20),
+        compiler_params=limits(36),
     )(ranks, query, *chunks, *extra)
 
 
@@ -383,12 +398,13 @@
     tokens = q_codes.shape[0]
     span = tokens * count
 
+    def place(chips, cores):
+        chip, core = rank // 2, rank % 2
+        chip = (chip + chips * (1 - 2 * core)) % (count // 2)
+        return chip * 2 + (core + cores) % 2
+
     def ranks(*steps):
-        chip, core = rank // 2, rank % 2
-        listed = [rank]
-        for chips, cores in steps:
-            listed.append((chip + chips) % (count // 2) * 2 + (core + cores) % 2)
-        return jnp.stack(listed).astype(jnp.int32)
+        return jnp.stack([rank, *(place(*step) for step in steps)]).astype(jnp.int32)
 
     def exchange(value):
         return lax.all_to_all(value, "seq", split_axis=0, concat_axis=0, tiled=True)
@@ -399,26 +415,23 @@
     packed, inner, decayed, before, fades = prepare_rest(q_codes, q_exps.T, *lin, seq_count)
     arrived = exchange(packed)
     own = after(own, packed)
-    below = ring(own, 2)
-    above = ring(own, -2)
+    onward = [(i + 2 - i % 2 * 4) % count for i in range(count)]
+    first = lax.ppermute(own, "head", list(enumerate(onward)))
+    second = lax.ppermute(own, "head", [(to, i) for i, to in enumerate(onward)])
     partner = core_swap(own)
-    arrived = after(arrived, below, above)
-    outward = jnp.where(rank % 2 == 0, below, above)
-    far = lax.ppermute(
-        outward, "head", [(i, (i + 2 - i % 2 * 4) % count) for i in range(count)]
-    )
-    below_other = core_swap(below)
-    above_other = core_swap(above)
-    state = attend(ranks((0, 0), (0, 1)), arrived, [own, partner], None, span)
-    entering = entering_states(arrived, tokens)
-    far_other = core_swap(after(far, state[0]))
+    far = lax.ppermute(first, "head", list(enumerate(onward)))
+    far_other = lax.ppermute(first, "head", [(i, to ^ 1) for i, to in enumerate(onward)])
+    arrived = after(arrived, first, second)
+    first_other = core_swap(first)
+    second_other = core_swap(second)
     state = attend(
-        ranks((-1, 0), (-1, 1), (1, 0), (1, 1)),
+        ranks((0, 0), (0, 1), (-1, 0), (1, 1), (1, 0), (-1, 1)),
         arrived,
-        [below, below_other, above, above_other],
-        state,
+        [own, partner, first, first_other, second, second_other],
+        None,
         span,
     )
+    entering = entering_states(arrived, tokens)
     attended = attend(
         ranks((2, 0), (2, 1)), arrived, [far, far_other], state, span, tail=entering
     )

time: 139 us -> 132 us (0.950)
  Pallas kernels: 41.2 us -> 37.3 us
  local copies, waits for them, and re-layouts: 2.29 us -> 0.1 us
  waiting for transfers between devices: 43 us -> 45.1 us
  blocking collectives: 27.8 us -> 25.8 us
    pallas_call x3 -> x2, Pallas kernels: 29.7 us -> 26.2 us  [attend(): pl.pallas_call(kernel, in_specs=[SMEM, VMEM] + [ANY] * chunk_count + [VME...]
    ppermute x3 -> x4, waiting for transfers between devices: 18 us -> 20.8 us  [the longest x1 18.2 us: shards(): first = lax.ppermute(own, 'head', list(enumerate(onward)))]
    unnamed x12 -> x8, local copies, waits for them, and re-layouts: 2.21 us -> 0.02 us
    all_to_all x1, blocking collectives: 27.8 us -> 25.8 us  [exchange(): return lax.all_to_all(value, 'seq', split_axis=0, concat_axis=0, tiled=True)]
    ppermute x3 -> x4, starting transfers between devices: 4.81 us -> 4.59 us  [the longest x1 1.66 us: shards(): second = lax.ppermute(own, 'head', [(to, i) for i, to in enumerate(onward)])]
  transfers between devices with their start and end apart: 9 -> 9, of which waited for: 4 -> 6; matrix products, arithmetic and copies ran while one was open for 1% -> 0% of each run, Pallas kernels for 20% -> 19%
where the time goes in v1:
time: 132 us; the launch traced here: 131 us
  waiting for transfers between devices  45.1 us (34%)
  Pallas kernels  37.3 us (28%)
  blocking collectives  25.8 us (20%)
  starting transfers between devices  21.6 us (16%)
    pallas_call x2, Pallas kernels, attend(): pl.pallas_call(kernel, in_specs=[SMEM, VMEM] + [ANY] * chunk_count + [VME...  26.2 us
    all_to_all x1, blocking collectives, exchange(): return lax.all_to_all(value, 'seq', split_axis=0, concat_axis=0, tiled=True)  25.8 us
    all_to_all x2, waiting for transfers between devices, exchange(): return lax.all_to_all(value, 'seq', split_axis=0, concat_axis=0, tiled=True)  23.8 us
    ppermute x1, waiting for transfers between devices, shards(): first = lax.ppermute(own, 'head', list(enumerate(onward)))  18.2 us
    all_to_all x2, starting transfers between devices, exchange(): return lax.all_to_all(value, 'seq', split_axis=0, concat_axis=0, tiled=True)  16.4 us
    pallas_call x1, Pallas kernels, prepare_rest(): pl.pallas_call(kernel, in_specs=[WHOLE] * 6, out_specs=[VMEM] * 5, out_sh...  6.61 us
    pallas_call x1, Pallas kernels, prepare(): pl.pallas_call(kernel, in_specs=[WHOLE] * (2 * count), out_specs=VMEM, ou...  2.65 us
  transfers between devices with their start and end apart: 9, of which 6 were waited for; matrix products, arithmetic and copies ran while one was open for 0% of the time, Pallas kernels for 19%

profile of v1, /device:TPU:32, one launch (start us, length us, event | category | flops | bytes accessed | tf_op | source)
XLA Modules:
  0.0 130.6 jit_solution(16069568854453938988)
XLA Ops:
  0.6 2.7 %shard_map.113 = bf16[32,128,128]{2,1,0:T(8,128)(2,1)} custom-call(bf16[64,4096]{1,0:T(8,128)(2,1)} %refs_0_.1, bf16[64,4096]{1,0:T(8,128)(2,1)} %refs_1_.1, s32[32,64]{1,0:T(8,128)} %bitcast.13, s32[32,64]{1,0:T(8,128)} %bitcast.14), custom_call_target="tpu_custom_call" | custom-call | tf_op jit(solution)/shard_map/pallas_call | solution.py:49
  3.3 11.2 %all-to-all-start.1 = ((bf16[32,128,128]{2,1,0:T(8,128)(2,1)}), bf16[32,128,128]{2,1,0:T(8,128)(2,1)S(1)}, u32[]{:S(2)}, u32[]{:S(2)}) async-start(bf16[32,128,128]{2,1,0:T(8,128)(2,1)} %shard_map.113), calls=%async_computation.1 | async-start | bytes 2097152 | tf_op jit(solution)/shard_map/all_to_all | solution.py:410
  14.5 6.6 %shard_map.114 = (bf16[32,96,128]{2,1,0:T(8,128)(2,1)}, f32[512,512]{1,0:T(8,128)}, bf16[512,512]{1,0:T(8,128)(2,1)}, f32[4,4,128,128]{3,2,1,0:T(8,128)}, f32[16,128]{1,0:T(8,128)}) custom-call(bf16[64,4096]{1,0:T(8,128)(2,1)} %code_ref.1, s32[32,64]{1,0:T(8,128)} %bitcast.15, bf16[512,512]{1,0:T(8,128)(2,1)} %q_ref, bf16[512,512]{1,0:T(8,128)(2,1)} %k_ref, ...), custom_call_target="tpu_custom_call" | custom-call | flops 4000000000 | bytes 6291456 | tf_op jit(solution)/shard_map/pallas_call | solution.py:318
  21.1 21.9 %all-to-all-done.1.refs_2_ = bf16[32,128,128]{2,1,0:T(8,128)(2,1)S(1)} async-done(((bf16[32,128,128]{2,1,0:T(8,128)(2,1)}), bf16[32,128,128]{2,1,0:T(8,128)(2,1)S(1)}, u32[]{:S(2)}, u32[]{:S(2)}) %all-to-all-start.1) | async-done | bytes 1048608 | tf_op jit(solution)/shard_map/all_to_all | solution.py:410
  43.0 1.6 %collective-permute-start = (bf16[32,128,128]{2,1,0:T(8,128)(2,1)S(1)}, bf16[32,128,128]{2,1,0:T(8,128)(2,1)S(1)}, u32[]{:S(2)}, u32[]{:S(2)}) collective-permute-start(bf16[32,128,128]{2,1,0:T(8,128)(2,1)S(1)} %all-to-all-done.1.refs_2_), channel_id=1, source_target_pairs={{0,2},{1,7},{2,4},{3,1},{4,6},{5,3},{6,0},{7,5},{8,10},{9,15},{10,... | collective-permute-start | bytes 3145736 | tf_op jit(solution)/shard_map/ppermute | solution.py:419
  44.6 1.7 %collective-permute-start.1 = (bf16[32,128,128]{2,1,0:T(8,128)(2,1)S(1)}, bf16[32,128,128]{2,1,0:T(8,128)(2,1)}, u32[]{:S(2)}, u32[]{:S(2)}) collective-permute-start(bf16[32,128,128]{2,1,0:T(8,128)(2,1)S(1)} %all-to-all-done.1.refs_2_), channel_id=1, source_target_pairs={{2,0},{7,1},{4,2},{1,3},{6,4},{3,5},{0,6},{5,7},{10,8},{15,9},{12,... | collective-permute-start | bytes 3145736 | tf_op jit(solution)/shard_map/ppermute | solution.py:420
  46.2 5.2 %all-to-all-start = ((bf16[32,96,128]{2,1,0:T(8,128)(2,1)}), bf16[32,96,128]{2,1,0:T(8,128)(2,1)S(1)}, u32[]{:S(2)}, u32[]{:S(2)}) async-start(bf16[32,96,128]{2,1,0:T(8,128)(2,1)} %get-tuple-element.20), calls=%async_computation | async-start | bytes 1572864 | tf_op jit(solution)/shard_map/all_to_all | solution.py:410
  51.4 0.1 collective-permute-start.4
  51.5 18.2 %collective-permute-done.refs_4_ = bf16[32,128,128]{2,1,0:T(8,128)(2,1)S(1)} collective-permute-done((bf16[32,128,128]{2,1,0:T(8,128)(2,1)S(1)}, bf16[32,128,128]{2,1,0:T(8,128)(2,1)S(1)}, u32[]{:S(2)}, u32[]{:S(2)}) %collective-permute-start) | collective-permute-done | bytes 1048608 | tf_op jit(solution)/shard_map/ppermute | solution.py:419
  69.7 0.0 collective-permute-start.5
  69.7 0.0 collective-permute-done.1.refs_6_
  69.7 0.5 collective-permute-start.6
  70.2 0.0 collective-permute-start.2
  70.2 1.4 %collective-permute-start.3 = (bf16[32,128,128]{2,1,0:T(8,128)(2,1)S(1)}, bf16[32,128,128]{2,1,0:T(8,128)(2,1)}, u32[]{:S(2)}, u32[]{:S(2)}) collective-permute-start(bf16[32,128,128]{2,1,0:T(8,128)(2,1)S(1)} %collective-permute-done.refs_4_), channel_id=1, source_target_pairs={{0,3},{1,6},{2,5},{3,0},{4,7},{5,2},{6,1},{7,4},{8,11},{9,14},{10,... | collective-permute-start | bytes 3145736 | tf_op jit(solution)/shard_map/ppermute | solution.py:423
  71.6 0.1 stack.44.refs_0_
  71.7 0.1 pad_add_fusion.refs_0_
  71.7 1.9 %all-to-all-done.refs_1_.in_ref = bf16[32,96,128]{2,1,0:T(8,128)(2,1)S(1)} async-done(((bf16[32,96,128]{2,1,0:T(8,128)(2,1)}), bf16[32,96,128]{2,1,0:T(8,128)(2,1)S(1)}, u32[]{:S(2)}, u32[]{:S(2)}) %all-to-all-start) | async-done | bytes 786464 | tf_op jit(solution)/shard_map/all_to_all | solution.py:410
  73.6 0.1 shard_map.116.refs_7_
  73.7 0.0 collective-permute-done.4.refs_3_
  73.7 0.2 collective-permute-done.5.refs_5_
  73.9 0.3 collective-permute-done.6.refs_7_
  74.2 18.6 %shard_map.115 = (f32[4,512]{1,0:T(4,128)S(1)}, f32[4,512]{1,0:T(4,128)S(1)}, f32[128,2048]{1,0:T(8,128)S(1)}) custom-call(s32[7]{0:T(128)S(1)} %stack.44.refs_0_, bf16[32,96,128]{2,1,0:T(8,128)(2,1)S(1)} %all-to-all-done.refs_1_.in_ref, bf16[32,128,128]{2,1,0:T(8,128)(2,1)S(1)} %all-to-all-done.1.refs_2_, ...), custom_call_target="tpu_custom_call" | custom-call | tf_op jit(solution)/shard_map/pallas_call | solution.py:237
  92.8 0.0 collective-permute-done.2.refs_2_
  92.8 2.6 %collective-permute-done.3.refs_3_ = bf16[32,128,128]{2,1,0:T(8,128)(2,1)} collective-permute-done((bf16[32,128,128]{2,1,0:T(8,128)(2,1)S(1)}, bf16[32,128,128]{2,1,0:T(8,128)(2,1)}, u32[]{:S(2)}, u32[]{:S(2)}) %collective-permute-start.3) | collective-permute-done | bytes 1048608 | tf_op jit(solution)/shard_map/ppermute | solution.py:423
  95.4 0.0 copy-start.1
  95.4 0.0 copy-start.2
  95.4 7.7 %shard_map.117 = bf16[32,80,128]{2,1,0:T(8,128)(2,1)S(1)} custom-call(s32[3]{0:T(128)S(1)} %pad_add_fusion.refs_0_, bf16[32,96,128]{2,1,0:T(8,128)(2,1)S(1)} %all-to-all-done.refs_1_.in_ref, bf16[32,128,128]{2,1,0:T(8,128)(2,1)} %collective-permute-done.2.refs_2_, bf16[32,128,128]{2,1,0:T(8,128)(2,1)} %collective-permute-done.3.refs_3_, ...), custom_call_target="tpu_custom_call" | custom-call | tf_op jit(solution)/shard_map/pallas_call | solution.py:237
  103.1 0.0 copy-start
  103.1 0.0 copy-start.3
  103.1 25.8 %all_to_all.15.in_ref = bf16[32,80,128]{2,1,0:T(8,128)(2,1)S(1)} all-to-all(bf16[32,80,128]{2,1,0:T(8,128)(2,1)S(1)} %shard_map.117), channel_id=1, replica_groups=mesh['seq'=32,'head'=8] {'seq'}, dimensions={0} | all-to-all | bytes 1310720 | tf_op jit(solution)/shard_map/all_to_all | solution.py:410
  128.8 0.0 copy-done.1
  128.8 0.0 copy-done.2
  128.8 0.0 copy-done
  128.9 0.0 copy-done.3
  128.9 1.7 %shard_map.118 = (bf16[64,4096]{1,0:T(8,128)(2,1)}, bf16[512,512]{1,0:T(8,128)(2,1)}) custom-call(bf16[32,80,128]{2,1,0:T(8,128)(2,1)S(1)} %all_to_all.15.in_ref, f32[512,512]{1,0:T(8,128)S(1)} %copy-done, bf16[512,512]{1,0:T(8,128)(2,1)S(1)} %copy-done.2, f32[4,4,128,128]{3,2,1,0:T(8,128)S(1)} %copy-done.1, f32[16,128]{1,0:T(8,128)S(1)} %copy-done.3), custom_call_target="tpu_custom_call" | custom-call | tf_op jit(solution)/shard_map/pallas_call | solution.py:380
Async XLA Ops:
  3.3 39.7 %all-to-all-start.1 = ((bf16[32,128,128]{2,1,0:T(8,128)(2,1)}), bf16[32,128,128]{2,1,0:T(8,128)(2,1)S(1)}, u32[]{:S(2)}, u32[]{:S(2)}) async-start(bf16[32,128,128]{2,1,0:T(8,128)(2,1)} %shard_map.113), calls=%async_computation.1 | async-start | bytes 2097152 | tf_op jit(solution)/shard_map/all_to_all | solution.py:410
  43.0 26.7 %collective-permute-start = (bf16[32,128,128]{2,1,0:T(8,128)(2,1)S(1)}, bf16[32,128,128]{2,1,0:T(8,128)(2,1)S(1)}, u32[]{:S(2)}, u32[]{:S(2)}) collective-permute-start(bf16[32,128,128]{2,1,0:T(8,128)(2,1)S(1)} %all-to-all-done.1.refs_2_), channel_id=1, source_target_pairs={{0,2},{1,7},{2,4},{3,1},{4,6},{5,3},{6,0},{7,5},{8,10},{9,15},{10,... | collective-permute-start | bytes 3145736 | tf_op jit(solution)/shard_map/ppermute | solution.py:419
  44.6 25.1 %collective-permute-start.1 = (bf16[32,128,128]{2,1,0:T(8,128)(2,1)S(1)}, bf16[32,128,128]{2,1,0:T(8,128)(2,1)}, u32[]{:S(2)}, u32[]{:S(2)}) collective-permute-start(bf16[32,128,128]{2,1,0:T(8,128)(2,1)S(1)} %all-to-all-done.1.refs_2_), channel_id=1, source_target_pairs={{2,0},{7,1},{4,2},{1,3},{6,4},{3,5},{0,6},{5,7},{10,8},{15,9},{12,... | collective-permute-start | bytes 3145736 | tf_op jit(solution)/shard_map/ppermute | solution.py:420
  46.2 27.4 %all-to-all-start = ((bf16[32,96,128]{2,1,0:T(8,128)(2,1)}), bf16[32,96,128]{2,1,0:T(8,128)(2,1)S(1)}, u32[]{:S(2)}, u32[]{:S(2)}) async-start(bf16[32,96,128]{2,1,0:T(8,128)(2,1)} %get-tuple-element.20), calls=%async_computation | async-start | bytes 1572864 | tf_op jit(solution)/shard_map/all_to_all | solution.py:410
  51.4 22.3 %collective-permute-start.4 = (bf16[32,128,128]{2,1,0:T(8,128)(2,1)S(1)}, bf16[32,128,128]{2,1,0:T(8,128)(2,1)}, u32[]{:S(2)}, u32[]{:S(2)}) collective-permute-start(bf16[32,128,128]{2,1,0:T(8,128)(2,1)S(1)} %all-to-all-done.1.refs_2_), channel_id=1, source_target_pairs={{0,1},{1,0},{2,3},{3,2},{4,5},{5,4},{6,7},{7,6},{8,9},{9,8},{10,11... | collective-permute-start | bytes 3145736 | tf_op jit(solution)/shard_map/ppermute | solution.py:26
  69.7 4.2 %collective-permute-start.5 = (bf16[32,128,128]{2,1,0:T(8,128)(2,1)S(1)}, bf16[32,128,128]{2,1,0:T(8,128)(2,1)}, u32[]{:S(2)}, u32[]{:S(2)}) collective-permute-start(bf16[32,128,128]{2,1,0:T(8,128)(2,1)S(1)} %collective-permute-done.refs_4_), channel_id=1, source_target_pairs={{0,1},{1,0},{2,3},{3,2},{4,5},{5,4},{6,7},{7,6},{8,9},{9,8},{10,11... | collective-permute-start | bytes 3145736 | tf_op jit(solution)/shard_map/ppermute | solution.py:26
  69.7 4.5 %collective-permute-start.6 = (bf16[32,128,128]{2,1,0:T(8,128)(2,1)}, bf16[32,128,128]{2,1,0:T(8,128)(2,1)}, u32[]{:S(2)}, u32[]{:S(2)}) collective-permute-start(bf16[32,128,128]{2,1,0:T(8,128)(2,1)} %collective-permute-done.1.refs_6_), channel_id=1, source_target_pairs={{0,1},{1,0},{2,3},{3,2},{4,5},{5,4},{6,7},{7,6},{8,9},{9,8},{10,11... | collective-permute-start | bytes 3145736 | tf_op jit(solution)/shard_map/ppermute | solution.py:26
  70.2 22.6 %collective-permute-start.2 = (bf16[32,128,128]{2,1,0:T(8,128)(2,1)S(1)}, bf16[32,128,128]{2,1,0:T(8,128)(2,1)}, u32[]{:S(2)}, u32[]{:S(2)}) collective-permute-start(bf16[32,128,128]{2,1,0:T(8,128)(2,1)S(1)} %collective-permute-done.refs_4_), channel_id=1, source_target_pairs={{0,2},{1,7},{2,4},{3,1},{4,6},{5,3},{6,0},{7,5},{8,10},{9,15},{10,... | collective-permute-start | bytes 3145736 | tf_op jit(solution)/shard_map/ppermute | solution.py:422
  70.2 25.2 %collective-permute-start.3 = (bf16[32,128,128]{2,1,0:T(8,128)(2,1)S(1)}, bf16[32,128,128]{2,1,0:T(8,128)(2,1)}, u32[]{:S(2)}, u32[]{:S(2)}) collective-permute-start(bf16[32,128,128]{2,1,0:T(8,128)(2,1)S(1)} %collective-permute-done.refs_4_), channel_id=1, source_target_pairs={{0,3},{1,6},{2,5},{3,0},{4,7},{5,2},{6,1},{7,4},{8,11},{9,14},{10,... | collective-permute-start | bytes 3145736 | tf_op jit(solution)/shard_map/ppermute | solution.py:423
  95.4 33.4 %copy-start.1 = (f32[4,4,128,128]{3,2,1,0:T(8,128)S(1)}, f32[4,4,128,128]{3,2,1,0:T(8,128)}, u32[]{:S(2)}) copy-start(f32[4,4,128,128]{3,2,1,0:T(8,128)} %get-tuple-element.28.before_ref) | copy-start | bytes 3145732
  95.4 33.4 %copy-start.2 = (bf16[512,512]{1,0:T(8,128)(2,1)S(1)}, bf16[512,512]{1,0:T(8,128)(2,1)}, u32[]{:S(2)}) copy-start(bf16[512,512]{1,0:T(8,128)(2,1)} %get-tuple-element.27.decayed_ref) | copy-start | bytes 1572868
  103.1 25.8 %copy-start = (f32[512,512]{1,0:T(8,128)S(1)}, f32[512,512]{1,0:T(8,128)}, u32[]{:S(2)}) copy-start(f32[512,512]{1,0:T(8,128)} %get-tuple-element.26.inner_ref) | copy-start | bytes 3145732
  103.1 25.8 %copy-start.3 = (f32[16,128]{1,0:T(8,128)S(1)}, f32[16,128]{1,0:T(8,128)}, u32[]{:S(2)}) copy-start(f32[16,128]{1,0:T(8,128)} %get-tuple-element.29.fade_ref) | copy-start | bytes 24580

commit v2 on v1

--- a/solution.py
+++ b/solution.py
@@ -63,7 +63,6 @@
     per = TILE // key_dev
     tiles = rows // TILE
     order = [*range(0, tiles, 2), *range(tiles - 1, 0, -2)]
-    early = (order[0] + 1) * per
     chunk_count = len(chunks)
     pairs = chunk_count // 2
     scale = math.log2(math.e) / math.sqrt(head_dim)
@@ -78,7 +77,8 @@
         o_ref = refs.pop(0) if finish else None
         m_ref, l_ref, acc_ref, held, sems, score_a, score_b = refs
         score_refs = (score_a, score_b)
-        parts = (slice(0, early), slice(early, seq_count))
+        ends = [0, *(min(seq_count, (max(order[: m + 1]) + 1) * per) for m in range(3))]
+        parts = [slice(ends[m], ends[m + 1]) for m in range(3)]
         copies = [
             [
                 pltpu.make_async_copy(sources[n].at[part], held.at[n, part], sems.at[n, m])
@@ -86,7 +86,7 @@
             ]
             for m, part in enumerate(parts)
         ]
-        for copy in copies[0] + copies[1]:
+        for copy in copies[0] + copies[1] + copies[2]:
             copy.start()
         if finish:
             o_ref[:, key_dev:, :] = tail_ref[...]
@@ -201,8 +201,8 @@
 
         def step(p, top):
             for at in range(1, tiles + 1):
-                if at == 1:
-                    arrive(p, 1)
+                if at in (1, 2):
+                    arrive(p, at)
                 if at == tiles:
                     arrive(p + 1, 0)
                 top = stage(p, at, top)
@@ -222,9 +222,9 @@
     ]
     scratch = [
         pltpu.VMEM((chunk_count, seq_count, 2 * key_dev, head_dim), jnp.bfloat16),
-        pltpu.SemaphoreType.DMA((chunk_count, 2)),
-        pltpu.VMEM((2 * rows, TILE), jnp.float32),
-        pltpu.VMEM((2 * rows, TILE), jnp.float32),
+        pltpu.SemaphoreType.DMA((chunk_count, 3)),
+        pltpu.VMEM((2 * (max(order[0::2]) + 1) * TILE, TILE), jnp.float32),
+        pltpu.VMEM((2 * (max(order[1::2]) + 1) * TILE, TILE), jnp.float32),
     ]
     if finish:
         out_rows = key_dev + tail.shape[1]
@@ -240,7 +240,7 @@
         out_specs=out_specs,
         out_shape=out_shape,
         scratch_shapes=scratch,
-        compiler_params=limits(36),
+        compiler_params=limits(25),
     )(ranks, query, *chunks, *extra)
 
 
@@ -360,27 +360,43 @@
     shares = soft_heads // heads
     share = rows - tokens
 
-    def kernel(in_ref, inner_ref, decayed_ref, before_ref, fade_ref, soft_ref, lin_ref):
+    def kernel(in_ref, inner_ref, decayed_ref, before_ref, fade_ref, *rest):
+        soft_out, lin_out, soft_ref, lin_ref, sems = rest
         for h in range(soft_heads):
             soft_ref[:, h * width : (h + 1) * width] = in_ref[h, :tokens, :]
+        copies = [pltpu.make_async_copy(soft_ref, soft_out, sems.at[blocks])]
+        copies[0].start()
+        enterings = []
         for h in range(heads):
-            cols = slice(h * head_dim, (h + 1) * head_dim)
             entering = in_ref[h * shares : (h + 1) * shares, tokens:, :].astype(jnp.float32)
-            entering = entering.reshape(head_dim, head_dim)
-            for n in range(blocks):
-                span = slice(n * STRETCH, (n + 1) * STRETCH)
+            enterings.append(entering.reshape(head_dim, head_dim))
+        for n in range(blocks):
+            span = slice(n * STRETCH, (n + 1) * STRETCH)
+            for h in range(heads):
+                cols = slice(h * head_dim, (h + 1) * head_dim)
                 fade = fade_ref[n * heads + h : n * heads + h + 1, :]
-                state = (fade * entering + before_ref[n, h]).astype(jnp.bfloat16)
+                state = (fade * enterings[h] + before_ref[n, h]).astype(jnp.bfloat16)
                 mixed = inner_ref[span, cols] + jnp.dot(
                     decayed_ref[span, cols], state, preferred_element_type=jnp.float32
                 )
                 mean = jnp.mean(mixed * mixed, axis=1, keepdims=True)
                 lin_ref[span, cols] = (mixed / jnp.sqrt(mean + 1e-06)).astype(jnp.bfloat16)
+            copies.append(
+                pltpu.make_async_copy(lin_ref.at[span], lin_out.at[span], sems.at[n])
+            )
+            copies[-1].start()
+        for copy in copies:
+            copy.wait()
 
     return pl.pallas_call(
         kernel,
         in_specs=[VMEM] * 5,
-        out_specs=[VMEM] * 2,
+        out_specs=[ANY] * 2,
+        scratch_shapes=[
+            pltpu.VMEM((tokens, soft_heads * width), jnp.bfloat16),
+            pltpu.VMEM(inner.shape, jnp.bfloat16),
+            pltpu.SemaphoreType.DMA((blocks + 1,)),
+        ],
         out_shape=[
             jax.ShapeDtypeStruct((tokens, soft_heads * width), jnp.bfloat16),
             jax.ShapeDtypeStruct(inner.shape, jnp.bfloat16),

time: 132 us -> 132 us (level)
  no operation moved by 1% of the time
where the time goes in v2:
time: 132 us; the launch traced here: 130 us
  waiting for transfers between devices  45 us (34%)
  Pallas kernels  37.1 us (28%)
  blocking collectives  25.7 us (19%)
  starting transfers between devices  21.6 us (16%)
    pallas_call x2, Pallas kernels, attend(): pl.pallas_call(kernel, in_specs=[SMEM, VMEM] + [ANY] * chunk_count + [VME...  26.3 us
    all_to_all x1, blocking collectives, exchange(): return lax.all_to_all(value, 'seq', split_axis=0, concat_axis=0, tiled=True)  25.7 us
    all_to_all x2, waiting for transfers between devices, exchange(): return lax.all_to_all(value, 'seq', split_axis=0, concat_axis=0, tiled=True)  23.8 us
    ppermute x1, waiting for transfers between devices, shards(): first = lax.ppermute(own, 'head', list(enumerate(onward)))  18.2 us
    all_to_all x2, starting transfers between devices, exchange(): return lax.all_to_all(value, 'seq', split_axis=0, concat_axis=0, tiled=True)  16.4 us
    pallas_call x1, Pallas kernels, prepare_rest(): pl.pallas_call(kernel, in_specs=[WHOLE] * 6, out_specs=[VMEM] * 5, out_sh...  6.61 us
    pallas_call x1, Pallas kernels, prepare(): pl.pallas_call(kernel, in_specs=[WHOLE] * (2 * count), out_specs=VMEM, ou...  2.65 us
  transfers between devices with their start and end apart: 9, of which 6 were waited for; matrix products, arithmetic and copies ran while one was open for 0% of the time, Pallas kernels for 19%

profile of v2, /device:TPU:32, one launch (start us, length us, event | category | flops | bytes accessed | tf_op | source)
XLA Modules:
  0.0 130.5 jit_solution(3335790422843330841)
XLA Ops:
  0.6 2.7 %shard_map.113 = bf16[32,128,128]{2,1,0:T(8,128)(2,1)} custom-call(bf16[64,4096]{1,0:T(8,128)(2,1)} %refs_0_.1, bf16[64,4096]{1,0:T(8,128)(2,1)} %refs_1_.1, s32[32,64]{1,0:T(8,128)} %bitcast.13, s32[32,64]{1,0:T(8,128)} %bitcast.14), custom_call_target="tpu_custom_call" | custom-call | tf_op jit(solution)/shard_map/pallas_call | solution.py:49
  3.3 11.2 %all-to-all-start.1 = ((bf16[32,128,128]{2,1,0:T(8,128)(2,1)}), bf16[32,128,128]{2,1,0:T(8,128)(2,1)S(1)}, u32[]{:S(2)}, u32[]{:S(2)}) async-start(bf16[32,128,128]{2,1,0:T(8,128)(2,1)} %shard_map.113), calls=%async_computation.1 | async-start | bytes 2097152 | tf_op jit(solution)/shard_map/all_to_all | solution.py:426
  14.5 6.6 %shard_map.114 = (bf16[32,96,128]{2,1,0:T(8,128)(2,1)}, f32[512,512]{1,0:T(8,128)}, bf16[512,512]{1,0:T(8,128)(2,1)}, f32[4,4,128,128]{3,2,1,0:T(8,128)}, f32[16,128]{1,0:T(8,128)}) custom-call(bf16[64,4096]{1,0:T(8,128)(2,1)} %code_ref.1, s32[32,64]{1,0:T(8,128)} %bitcast.15, bf16[512,512]{1,0:T(8,128)(2,1)} %q_ref, bf16[512,512]{1,0:T(8,128)(2,1)} %k_ref, ...), custom_call_target="tpu_custom_call" | custom-call | flops 4000000000 | bytes 6291456 | tf_op jit(solution)/shard_map/pallas_call | solution.py:318
  21.1 21.9 %all-to-all-done.1.refs_2_ = bf16[32,128,128]{2,1,0:T(8,128)(2,1)S(1)} async-done(((bf16[32,128,128]{2,1,0:T(8,128)(2,1)}), bf16[32,128,128]{2,1,0:T(8,128)(2,1)S(1)}, u32[]{:S(2)}, u32[]{:S(2)}) %all-to-all-start.1) | async-done | bytes 1048608 | tf_op jit(solution)/shard_map/all_to_all | solution.py:426
  43.0 1.6 %collective-permute-start = (bf16[32,128,128]{2,1,0:T(8,128)(2,1)S(1)}, bf16[32,128,128]{2,1,0:T(8,128)(2,1)S(1)}, u32[]{:S(2)}, u32[]{:S(2)}) collective-permute-start(bf16[32,128,128]{2,1,0:T(8,128)(2,1)S(1)} %all-to-all-done.1.refs_2_), channel_id=1, source_target_pairs={{0,2},{1,7},{2,4},{3,1},{4,6},{5,3},{6,0},{7,5},{8,10},{9,15},{10,... | collective-permute-start | bytes 3145736 | tf_op jit(solution)/shard_map/ppermute | solution.py:435
  44.6 1.7 %collective-permute-start.1 = (bf16[32,128,128]{2,1,0:T(8,128)(2,1)S(1)}, bf16[32,128,128]{2,1,0:T(8,128)(2,1)}, u32[]{:S(2)}, u32[]{:S(2)}) collective-permute-start(bf16[32,128,128]{2,1,0:T(8,128)(2,1)S(1)} %all-to-all-done.1.refs_2_), channel_id=1, source_target_pairs={{2,0},{7,1},{4,2},{1,3},{6,4},{3,5},{0,6},{5,7},{10,8},{15,9},{12,... | collective-permute-start | bytes 3145736 | tf_op jit(solution)/shard_map/ppermute | solution.py:436
  46.2 5.2 %all-to-all-start = ((bf16[32,96,128]{2,1,0:T(8,128)(2,1)}), bf16[32,96,128]{2,1,0:T(8,128)(2,1)S(1)}, u32[]{:S(2)}, u32[]{:S(2)}) async-start(bf16[32,96,128]{2,1,0:T(8,128)(2,1)} %get-tuple-element.20), calls=%async_computation | async-start | bytes 1572864 | tf_op jit(solution)/shard_map/all_to_all | solution.py:426
  51.4 0.1 collective-permute-start.4
  51.5 18.2 %collective-permute-done.refs_4_ = bf16[32,128,128]{2,1,0:T(8,128)(2,1)S(1)} collective-permute-done((bf16[32,128,128]{2,1,0:T(8,128)(2,1)S(1)}, bf16[32,128,128]{2,1,0:T(8,128)(2,1)S(1)}, u32[]{:S(2)}, u32[]{:S(2)}) %collective-permute-start) | collective-permute-done | bytes 1048608 | tf_op jit(solution)/shard_map/ppermute | solution.py:435
  69.7 0.0 collective-permute-start.5
  69.7 0.0 collective-permute-done.1.refs_6_
  69.7 0.5 collective-permute-start.6
  70.2 0.0 collective-permute-start.2
  70.2 1.4 %collective-permute-start.3 = (bf16[32,128,128]{2,1,0:T(8,128)(2,1)S(1)}, bf16[32,128,128]{2,1,0:T(8,128)(2,1)}, u32[]{:S(2)}, u32[]{:S(2)}) collective-permute-start(bf16[32,128,128]{2,1,0:T(8,128)(2,1)S(1)} %collective-permute-done.refs_4_), channel_id=1, source_target_pairs={{0,3},{1,6},{2,5},{3,0},{4,7},{5,2},{6,1},{7,4},{8,11},{9,14},{10,... | collective-permute-start | bytes 3145736 | tf_op jit(solution)/shard_map/ppermute | solution.py:439
  71.6 0.1 stack.44.refs_0_
  71.7 0.1 pad_add_fusion.refs_0_
  71.7 1.9 %all-to-all-done.refs_1_.in_ref = bf16[32,96,128]{2,1,0:T(8,128)(2,1)S(1)} async-done(((bf16[32,96,128]{2,1,0:T(8,128)(2,1)}), bf16[32,96,128]{2,1,0:T(8,128)(2,1)S(1)}, u32[]{:S(2)}, u32[]{:S(2)}) %all-to-all-start) | async-done | bytes 786464 | tf_op jit(solution)/shard_map/all_to_all | solution.py:426
  73.6 0.1 shard_map.116.refs_7_
  73.7 0.0 collective-permute-done.4.refs_3_
  73.7 0.2 collective-permute-done.5.refs_5_
  73.9 0.3 collective-permute-done.6.refs_7_
  74.2 18.6 %shard_map.115 = (f32[4,512]{1,0:T(4,128)S(1)}, f32[4,512]{1,0:T(4,128)S(1)}, f32[128,2048]{1,0:T(8,128)S(1)}) custom-call(s32[7]{0:T(128)S(1)} %stack.44.refs_0_, bf16[32,96,128]{2,1,0:T(8,128)(2,1)S(1)} %all-to-all-done.refs_1_.in_ref, bf16[32,128,128]{2,1,0:T(8,128)(2,1)S(1)} %all-to-all-done.1.refs_2_, ...), custom_call_target="tpu_custom_call" | custom-call | tf_op jit(solution)/shard_map/pallas_call | solution.py:237
  92.8 0.0 collective-permute-done.2.refs_2_
  92.8 2.6 %collective-permute-done.3.refs_3_ = bf16[32,128,128]{2,1,0:T(8,128)(2,1)} collective-permute-done((bf16[32,128,128]{2,1,0:T(8,128)(2,1)S(1)}, bf16[32,128,128]{2,1,0:T(8,128)(2,1)}, u32[]{:S(2)}, u32[]{:S(2)}) %collective-permute-start.3) | collective-permute-done | bytes 1048608 | tf_op jit(solution)/shard_map/ppermute | solution.py:439
  95.4 0.0 copy-start.1
  95.4 0.0 copy-start.2
  95.4 7.7 %shard_map.117 = bf16[32,80,128]{2,1,0:T(8,128)(2,1)S(1)} custom-call(s32[3]{0:T(128)S(1)} %pad_add_fusion.refs_0_, bf16[32,96,128]{2,1,0:T(8,128)(2,1)S(1)} %all-to-all-done.refs_1_.in_ref, bf16[32,128,128]{2,1,0:T(8,128)(2,1)} %collective-permute-done.2.refs_2_, bf16[32,128,128]{2,1,0:T(8,128)(2,1)} %collective-permute-done.3.refs_3_, ...), custom_call_target="tpu_custom_call" | custom-call | tf_op jit(solution)/shard_map/pallas_call | solution.py:237
  103.1 0.0 copy-start
  103.1 0.0 copy-start.3
  103.1 25.7 %all_to_all.15.in_ref = bf16[32,80,128]{2,1,0:T(8,128)(2,1)S(1)} all-to-all(bf16[32,80,128]{2,1,0:T(8,128)(2,1)S(1)} %shard_map.117), channel_id=1, replica_groups=mesh['seq'=32,'head'=8] {'seq'}, dimensions={0} | all-to-all | bytes 1310720 | tf_op jit(solution)/shard_map/all_to_all | solution.py:426
  128.9 0.0 copy-done.1
  128.9 0.0 copy-done.2
  128.9 0.0 copy-done
  128.9 0.0 copy-done.3
  128.9 1.5 %shard_map.118 = (bf16[64,4096]{1,0:T(8,128)(2,1)}, bf16[512,512]{1,0:T(8,128)(2,1)}) custom-call(bf16[32,80,128]{2,1,0:T(8,128)(2,1)S(1)} %all_to_all.15.in_ref, f32[512,512]{1,0:T(8,128)S(1)} %copy-done, bf16[512,512]{1,0:T(8,128)(2,1)S(1)} %copy-done.2, f32[4,4,128,128]{3,2,1,0:T(8,128)S(1)} %copy-done.1, f32[16,128]{1,0:T(8,128)S(1)} %copy-done.3), custom_call_target="tpu_custom_call" | custom-call | tf_op jit(solution)/shard_map/pallas_call | solution.py:391
Async XLA Ops:
  3.3 39.7 %all-to-all-start.1 = ((bf16[32,128,128]{2,1,0:T(8,128)(2,1)}), bf16[32,128,128]{2,1,0:T(8,128)(2,1)S(1)}, u32[]{:S(2)}, u32[]{:S(2)}) async-start(bf16[32,128,128]{2,1,0:T(8,128)(2,1)} %shard_map.113), calls=%async_computation.1 | async-start | bytes 2097152 | tf_op jit(solution)/shard_map/all_to_all | solution.py:426
  43.0 26.7 %collective-permute-start = (bf16[32,128,128]{2,1,0:T(8,128)(2,1)S(1)}, bf16[32,128,128]{2,1,0:T(8,128)(2,1)S(1)}, u32[]{:S(2)}, u32[]{:S(2)}) collective-permute-start(bf16[32,128,128]{2,1,0:T(8,128)(2,1)S(1)} %all-to-all-done.1.refs_2_), channel_id=1, source_target_pairs={{0,2},{1,7},{2,4},{3,1},{4,6},{5,3},{6,0},{7,5},{8,10},{9,15},{10,... | collective-permute-start | bytes 3145736 | tf_op jit(solution)/shard_map/ppermute | solution.py:435
  44.6 25.1 %collective-permute-start.1 = (bf16[32,128,128]{2,1,0:T(8,128)(2,1)S(1)}, bf16[32,128,128]{2,1,0:T(8,128)(2,1)}, u32[]{:S(2)}, u32[]{:S(2)}) collective-permute-start(bf16[32,128,128]{2,1,0:T(8,128)(2,1)S(1)} %all-to-all-done.1.refs_2_), channel_id=1, source_target_pairs={{2,0},{7,1},{4,2},{1,3},{6,4},{3,5},{0,6},{5,7},{10,8},{15,9},{12,... | collective-permute-start | bytes 3145736 | tf_op jit(solution)/shard_map/ppermute | solution.py:436
  46.2 27.4 %all-to-all-start = ((bf16[32,96,128]{2,1,0:T(8,128)(2,1)}), bf16[32,96,128]{2,1,0:T(8,128)(2,1)S(1)}, u32[]{:S(2)}, u32[]{:S(2)}) async-start(bf16[32,96,128]{2,1,0:T(8,128)(2,1)} %get-tuple-element.20), calls=%async_computation | async-start | bytes 1572864 | tf_op jit(solution)/shard_map/all_to_all | solution.py:426
  51.4 22.3 %collective-permute-start.4 = (bf16[32,128,128]{2,1,0:T(8,128)(2,1)S(1)}, bf16[32,128,128]{2,1,0:T(8,128)(2,1)}, u32[]{:S(2)}, u32[]{:S(2)}) collective-permute-start(bf16[32,128,128]{2,1,0:T(8,128)(2,1)S(1)} %all-to-all-done.1.refs_2_), channel_id=1, source_target_pairs={{0,1},{1,0},{2,3},{3,2},{4,5},{5,4},{6,7},{7,6},{8,9},{9,8},{10,11... | collective-permute-start | bytes 3145736 | tf_op jit(solution)/shard_map/ppermute | solution.py:26
  69.7 4.2 %collective-permute-start.5 = (bf16[32,128,128]{2,1,0:T(8,128)(2,1)S(1)}, bf16[32,128,128]{2,1,0:T(8,128)(2,1)}, u32[]{:S(2)}, u32[]{:S(2)}) collective-permute-start(bf16[32,128,128]{2,1,0:T(8,128)(2,1)S(1)} %collective-permute-done.refs_4_), channel_id=1, source_target_pairs={{0,1},{1,0},{2,3},{3,2},{4,5},{5,4},{6,7},{7,6},{8,9},{9,8},{10,11... | collective-permute-start | bytes 3145736 | tf_op jit(solution)/shard_map/ppermute | solution.py:26
  69.7 4.5 %collective-permute-start.6 = (bf16[32,128,128]{2,1,0:T(8,128)(2,1)}, bf16[32,128,128]{2,1,0:T(8,128)(2,1)}, u32[]{:S(2)}, u32[]{:S(2)}) collective-permute-start(bf16[32,128,128]{2,1,0:T(8,128)(2,1)} %collective-permute-done.1.refs_6_), channel_id=1, source_target_pairs={{0,1},{1,0},{2,3},{3,2},{4,5},{5,4},{6,7},{7,6},{8,9},{9,8},{10,11... | collective-permute-start | bytes 3145736 | tf_op jit(solution)/shard_map/ppermute | solution.py:26
  70.2 22.6 %collective-permute-start.2 = (bf16[32,128,128]{2,1,0:T(8,128)(2,1)S(1)}, bf16[32,128,128]{2,1,0:T(8,128)(2,1)}, u32[]{:S(2)}, u32[]{:S(2)}) collective-permute-start(bf16[32,128,128]{2,1,0:T(8,128)(2,1)S(1)} %collective-permute-done.refs_4_), channel_id=1, source_target_pairs={{0,2},{1,7},{2,4},{3,1},{4,6},{5,3},{6,0},{7,5},{8,10},{9,15},{10,... | collective-permute-start | bytes 3145736 | tf_op jit(solution)/shard_map/ppermute | solution.py:438
  70.2 25.2 %collective-permute-start.3 = (bf16[32,128,128]{2,1,0:T(8,128)(2,1)S(1)}, bf16[32,128,128]{2,1,0:T(8,128)(2,1)}, u32[]{:S(2)}, u32[]{:S(2)}) collective-permute-start(bf16[32,128,128]{2,1,0:T(8,128)(2,1)S(1)} %collective-permute-done.refs_4_), channel_id=1, source_target_pairs={{0,3},{1,6},{2,5},{3,0},{4,7},{5,2},{6,1},{7,4},{8,11},{9,14},{10,... | collective-permute-start | bytes 3145736 | tf_op jit(solution)/shard_map/ppermute | solution.py:439
  95.4 33.5 %copy-start.1 = (f32[4,4,128,128]{3,2,1,0:T(8,128)S(1)}, f32[4,4,128,128]{3,2,1,0:T(8,128)}, u32[]{:S(2)}) copy-start(f32[4,4,128,128]{3,2,1,0:T(8,128)} %get-tuple-element.28.before_ref) | copy-start | bytes 3145732
  95.4 33.5 %copy-start.2 = (bf16[512,512]{1,0:T(8,128)(2,1)S(1)}, bf16[512,512]{1,0:T(8,128)(2,1)}, u32[]{:S(2)}) copy-start(bf16[512,512]{1,0:T(8,128)(2,1)} %get-tuple-element.27.decayed_ref) | copy-start | bytes 1572868
  103.1 25.8 %copy-start = (f32[512,512]{1,0:T(8,128)S(1)}, f32[512,512]{1,0:T(8,128)}, u32[]{:S(2)}) copy-start(f32[512,512]{1,0:T(8,128)} %get-tuple-element.26.inner_ref) | copy-start | bytes 3145732
  103.1 25.8 %copy-start.3 = (f32[16,128]{1,0:T(8,128)S(1)}, f32[16,128]{1,0:T(8,128)}, u32[]{:S(2)}) copy-start(f32[16,128]{1,0:T(8,128)} %get-tuple-element.29.fade_ref) | copy-start | bytes 24580

commit v3 on v2

--- a/solution.py
+++ b/solution.py
@@ -438,7 +438,7 @@
     far = lax.ppermute(first, "head", list(enumerate(onward)))
     far_other = lax.ppermute(first, "head", [(i, to ^ 1) for i, to in enumerate(onward)])
     arrived = after(arrived, first, second)
-    first_other = core_swap(first)
+    first_other = core_swap(after(first, second))
     second_other = core_swap(second)
     state = attend(
         ranks((0, 0), (0, 1), (-1, 0), (1, 1), (1, 0), (-1, 1)),
@@ -447,7 +447,7 @@
         None,
         span,
     )
-    entering = entering_states(arrived, tokens)
+    entering = entering_states(after(arrived, state[0]), tokens)
     attended = attend(
         ranks((2, 0), (2, 1)), arrived, [far, far_other], state, span, tail=entering
     )

time: 132 us -> 131 us (level)
  waiting for transfers between devices: 45 us -> 43.4 us
    ppermute x1, waiting for transfers between devices: 18.2 us -> 0.01 us  [shards(): first = lax.ppermute(own, 'head', list(enumerate(onward)))]
    ppermute x1, waiting for transfers between devices: 0.01 us -> 15.8 us  [shards(): second = lax.ppermute(own, 'head', [(to, i) for i, to in enumerate(onward)])]
    ppermute x1, waiting for transfers between devices: 2.56 us -> 0.01 us  [shards(): lax.ppermute(first, 'head', [(i, to ^ 1) for i, to in enumerate(onward)])]
    ppermute x1, waiting for transfers between devices: 0.01 us -> 2.36 us  [shards(): far = lax.ppermute(first, 'head', list(enumerate(onward)))]
    ppermute x1, starting transfers between devices: 1.58 us -> 0.01 us  [shards(): first = lax.ppermute(own, 'head', list(enumerate(onward)))]
    all_to_all x2, waiting for transfers between devices: 23.8 us -> 25.2 us  [exchange(): return lax.all_to_all(value, 'seq', split_axis=0, concat_axis=0, tiled=True)]
    ppermute x1, starting transfers between devices: 1.66 us -> 3.02 us  [shards(): second = lax.ppermute(own, 'head', [(to, i) for i, to in enumerate(onward)])]
  transfers between devices with their start and end apart: 9 -> 9, of which waited for: 6 -> 4; matrix products, arithmetic and copies ran while one was open for 0% -> 0% of each run, Pallas kernels for 19% -> 19%
where the time goes in v3:
time: 131 us; the launch traced here: 130 us
  waiting for transfers between devices  43.4 us (33%)
  Pallas kernels  37.1 us (28%)
  blocking collectives  26.3 us (20%)
  starting transfers between devices  22.5 us (17%)
    pallas_call x2, Pallas kernels, attend(): pl.pallas_call(kernel, in_specs=[SMEM, VMEM] + [ANY] * chunk_count + [VME...  26.3 us
    all_to_all x1, blocking collectives, exchange(): return lax.all_to_all(value, 'seq', split_axis=0, concat_axis=0, tiled=True)  26.3 us
    all_to_all x2, waiting for transfers between devices, exchange(): return lax.all_to_all(value, 'seq', split_axis=0, concat_axis=0, tiled=True)  25.2 us
    all_to_all x2, starting transfers between devices, exchange(): return lax.all_to_all(value, 'seq', split_axis=0, concat_axis=0, tiled=True)  16.4 us
    ppermute x1, waiting for transfers between devices, shards(): second = lax.ppermute(own, 'head', [(to, i) for i, to in enumerate(onward)])  15.8 us
    pallas_call x1, Pallas kernels, prepare_rest(): pl.pallas_call(kernel, in_specs=[WHOLE] * 6, out_specs=[VMEM] * 5, out_sh...  6.61 us
    ppermute x1, starting transfers between devices, shards(): second = lax.ppermute(own, 'head', [(to, i) for i, to in enumerate(onward)])  3.02 us
    pallas_call x1, Pallas kernels, prepare(): pl.pallas_call(kernel, in_specs=[WHOLE] * (2 * count), out_specs=VMEM, ou...  2.65 us
  transfers between devices with their start and end apart: 9, of which 4 were waited for; matrix products, arithmetic and copies ran while one was open for 0% of the time, Pallas kernels for 19%

profile of v3, /device:TPU:32, one launch (start us, length us, event | category | flops | bytes accessed | tf_op | source)
XLA Modules:
  0.0 130.4 jit_solution(15480543768912547214)
XLA Ops:
  0.6 2.7 %shard_map.113 = bf16[32,128,128]{2,1,0:T(8,128)(2,1)} custom-call(bf16[64,4096]{1,0:T(8,128)(2,1)} %refs_0_.1, bf16[64,4096]{1,0:T(8,128)(2,1)} %refs_1_.1, s32[32,64]{1,0:T(8,128)} %bitcast.13, s32[32,64]{1,0:T(8,128)} %bitcast.14), custom_call_target="tpu_custom_call" | custom-call | tf_op jit(solution)/shard_map/pallas_call | solution.py:49
  3.3 11.2 %all-to-all-start.1 = ((bf16[32,128,128]{2,1,0:T(8,128)(2,1)}), bf16[32,128,128]{2,1,0:T(8,128)(2,1)S(1)}, u32[]{:S(2)}, u32[]{:S(2)}) async-start(bf16[32,128,128]{2,1,0:T(8,128)(2,1)} %shard_map.113), calls=%async_computation.1 | async-start | bytes 2097152 | tf_op jit(solution)/shard_map/all_to_all | solution.py:426
  14.5 6.6 %shard_map.114 = (bf16[32,96,128]{2,1,0:T(8,128)(2,1)}, f32[512,512]{1,0:T(8,128)}, bf16[512,512]{1,0:T(8,128)(2,1)}, f32[4,4,128,128]{3,2,1,0:T(8,128)}, f32[16,128]{1,0:T(8,128)}) custom-call(bf16[64,4096]{1,0:T(8,128)(2,1)} %code_ref.1, s32[32,64]{1,0:T(8,128)} %bitcast.15, bf16[512,512]{1,0:T(8,128)(2,1)} %q_ref, bf16[512,512]{1,0:T(8,128)(2,1)} %k_ref, ...), custom_call_target="tpu_custom_call" | custom-call | flops 4000000000 | bytes 6291456 | tf_op jit(solution)/shard_map/pallas_call | solution.py:318
  21.1 21.9 %all-to-all-done.1.refs_2_ = bf16[32,128,128]{2,1,0:T(8,128)(2,1)S(1)} async-done(((bf16[32,128,128]{2,1,0:T(8,128)(2,1)}), bf16[32,128,128]{2,1,0:T(8,128)(2,1)S(1)}, u32[]{:S(2)}, u32[]{:S(2)}) %all-to-all-start.1) | async-done | bytes 1048608 | tf_op jit(solution)/shard_map/all_to_all | solution.py:426
  43.0 3.0 %collective-permute-start.1 = (bf16[32,128,128]{2,1,0:T(8,128)(2,1)S(1)}, bf16[32,128,128]{2,1,0:T(8,128)(2,1)}, u32[]{:S(2)}, u32[]{:S(2)}) collective-permute-start(bf16[32,128,128]{2,1,0:T(8,128)(2,1)S(1)} %all-to-all-done.1.refs_2_), channel_id=1, source_target_pairs={{2,0},{7,1},{4,2},{1,3},{6,4},{3,5},{0,6},{5,7},{10,8},{15,9},{12,... | collective-permute-start | bytes 3145736 | tf_op jit(solution)/shard_map/ppermute | solution.py:436
  46.0 0.0 collective-permute-start
  46.0 5.2 %all-to-all-start = ((bf16[32,96,128]{2,1,0:T(8,128)(2,1)}), bf16[32,96,128]{2,1,0:T(8,128)(2,1)S(1)}, u32[]{:S(2)}, u32[]{:S(2)}) async-start(bf16[32,96,128]{2,1,0:T(8,128)(2,1)} %get-tuple-element.22), calls=%async_computation | async-start | bytes 1572864 | tf_op jit(solution)/shard_map/all_to_all | solution.py:426
  51.2 0.1 collective-permute-start.4
  51.3 15.8 %collective-permute-done.1.refs_6_ = bf16[32,128,128]{2,1,0:T(8,128)(2,1)} collective-permute-done((bf16[32,128,128]{2,1,0:T(8,128)(2,1)S(1)}, bf16[32,128,128]{2,1,0:T(8,128)(2,1)}, u32[]{:S(2)}, u32[]{:S(2)}) %collective-permute-start.1) | collective-permute-done | bytes 1048608 | tf_op jit(solution)/shard_map/ppermute | solution.py:436
  67.1 0.0 collective-permute-done.refs_4_
  67.1 0.0 collective-permute-start.6
  67.1 0.5 collective-permute-start.5
  67.6 1.2 collective-permute-start.3
  68.8 1.3 collective-permute-start.2
  70.1 0.1 stack.44.refs_0_
  70.2 0.1 pad_add_fusion.refs_0_
  70.3 3.3 %all-to-all-done.refs_1_.in_ref = bf16[32,96,128]{2,1,0:T(8,128)(2,1)S(1)} async-done(((bf16[32,96,128]{2,1,0:T(8,128)(2,1)}), bf16[32,96,128]{2,1,0:T(8,128)(2,1)S(1)}, u32[]{:S(2)}, u32[]{:S(2)}) %all-to-all-start) | async-done | bytes 786464 | tf_op jit(solution)/shard_map/all_to_all | solution.py:426
  73.6 0.0 collective-permute-done.4.refs_3_
  73.6 0.0 collective-permute-done.6.refs_7_
  73.6 0.0 collective-permute-done.5.refs_5_
  73.6 18.6 %shard_map.115 = (f32[4,512]{1,0:T(4,128)S(1)}, f32[4,512]{1,0:T(4,128)S(1)}, f32[128,2048]{1,0:T(8,128)S(1)}) custom-call(s32[7]{0:T(128)S(1)} %stack.44.refs_0_, bf16[32,96,128]{2,1,0:T(8,128)(2,1)S(1)} %all-to-all-done.refs_1_.in_ref, bf16[32,128,128]{2,1,0:T(8,128)(2,1)S(1)} %all-to-all-done.1.refs_2_, ...), custom_call_target="tpu_custom_call" | custom-call | tf_op jit(solution)/shard_map/pallas_call | solution.py:237
  92.2 0.1 shard_map.116.refs_7_
  92.3 0.0 collective-permute-done.3.refs_3_
  92.3 2.4 %collective-permute-done.2.refs_2_ = bf16[32,128,128]{2,1,0:T(8,128)(2,1)} collective-permute-done((bf16[32,128,128]{2,1,0:T(8,128)(2,1)S(1)}, bf16[32,128,128]{2,1,0:T(8,128)(2,1)}, u32[]{:S(2)}, u32[]{:S(2)}) %collective-permute-start.2) | collective-permute-done | bytes 1048608 | tf_op jit(solution)/shard_map/ppermute | solution.py:438
  94.7 0.0 copy-start.1
  94.7 0.0 copy-start.2
  94.7 7.7 %shard_map.117 = bf16[32,80,128]{2,1,0:T(8,128)(2,1)S(1)} custom-call(s32[3]{0:T(128)S(1)} %pad_add_fusion.refs_0_, bf16[32,96,128]{2,1,0:T(8,128)(2,1)S(1)} %all-to-all-done.refs_1_.in_ref, bf16[32,128,128]{2,1,0:T(8,128)(2,1)} %collective-permute-done.2.refs_2_, bf16[32,128,128]{2,1,0:T(8,128)(2,1)} %collective-permute-done.3.refs_3_, ...), custom_call_target="tpu_custom_call" | custom-call | tf_op jit(solution)/shard_map/pallas_call | solution.py:237
  102.4 0.0 copy-start
  102.4 0.0 copy-start.3
  102.4 26.3 %all_to_all.15.in_ref = bf16[32,80,128]{2,1,0:T(8,128)(2,1)S(1)} all-to-all(bf16[32,80,128]{2,1,0:T(8,128)(2,1)S(1)} %shard_map.117), channel_id=1, replica_groups=mesh['seq'=32,'head'=8] {'seq'}, dimensions={0} | all-to-all | bytes 1310720 | tf_op jit(solution)/shard_map/all_to_all | solution.py:426
  128.7 0.0 copy-done.1
  128.7 0.0 copy-done.2
  128.7 0.0 copy-done
  128.7 0.0 copy-done.3
  128.7 1.5 %shard_map.118 = (bf16[64,4096]{1,0:T(8,128)(2,1)}, bf16[512,512]{1,0:T(8,128)(2,1)}) custom-call(bf16[32,80,128]{2,1,0:T(8,128)(2,1)S(1)} %all_to_all.15.in_ref, f32[512,512]{1,0:T(8,128)S(1)} %copy-done, bf16[512,512]{1,0:T(8,128)(2,1)S(1)} %copy-done.2, f32[4,4,128,128]{3,2,1,0:T(8,128)S(1)} %copy-done.1, f32[16,128]{1,0:T(8,128)S(1)} %copy-done.3), custom_call_target="tpu_custom_call" | custom-call | tf_op jit(solution)/shard_map/pallas_call | solution.py:391
Async XLA Ops:
  3.3 39.7 %all-to-all-start.1 = ((bf16[32,128,128]{2,1,0:T(8,128)(2,1)}), bf16[32,128,128]{2,1,0:T(8,128)(2,1)S(1)}, u32[]{:S(2)}, u32[]{:S(2)}) async-start(bf16[32,128,128]{2,1,0:T(8,128)(2,1)} %shard_map.113), calls=%async_computation.1 | async-start | bytes 2097152 | tf_op jit(solution)/shard_map/all_to_all | solution.py:426
  43.0 24.1 %collective-permute-start.1 = (bf16[32,128,128]{2,1,0:T(8,128)(2,1)S(1)}, bf16[32,128,128]{2,1,0:T(8,128)(2,1)}, u32[]{:S(2)}, u32[]{:S(2)}) collective-permute-start(bf16[32,128,128]{2,1,0:T(8,128)(2,1)S(1)} %all-to-all-done.1.refs_2_), channel_id=1, source_target_pairs={{2,0},{7,1},{4,2},{1,3},{6,4},{3,5},{0,6},{5,7},{10,8},{15,9},{12,... | collective-permute-start | bytes 3145736 | tf_op jit(solution)/shard_map/ppermute | solution.py:436
  46.0 21.1 %collective-permute-start = (bf16[32,128,128]{2,1,0:T(8,128)(2,1)S(1)}, bf16[32,128,128]{2,1,0:T(8,128)(2,1)S(1)}, u32[]{:S(2)}, u32[]{:S(2)}) collective-permute-start(bf16[32,128,128]{2,1,0:T(8,128)(2,1)S(1)} %all-to-all-done.1.refs_2_), channel_id=1, source_target_pairs={{0,2},{1,7},{2,4},{3,1},{4,6},{5,3},{6,0},{7,5},{8,10},{9,15},{10,... | collective-permute-start | bytes 3145736 | tf_op jit(solution)/shard_map/ppermute | solution.py:435
  46.0 27.6 %all-to-all-start = ((bf16[32,96,128]{2,1,0:T(8,128)(2,1)}), bf16[32,96,128]{2,1,0:T(8,128)(2,1)S(1)}, u32[]{:S(2)}, u32[]{:S(2)}) async-start(bf16[32,96,128]{2,1,0:T(8,128)(2,1)} %get-tuple-element.22), calls=%async_computation | async-start | bytes 1572864 | tf_op jit(solution)/shard_map/all_to_all | solution.py:426
  51.2 22.4 %collective-permute-start.4 = (bf16[32,128,128]{2,1,0:T(8,128)(2,1)S(1)}, bf16[32,128,128]{2,1,0:T(8,128)(2,1)}, u32[]{:S(2)}, u32[]{:S(2)}) collective-permute-start(bf16[32,128,128]{2,1,0:T(8,128)(2,1)S(1)} %all-to-all-done.1.refs_2_), channel_id=1, source_target_pairs={{0,1},{1,0},{2,3},{3,2},{4,5},{5,4},{6,7},{7,6},{8,9},{9,8},{10,11... | collective-permute-start | bytes 3145736 | tf_op jit(solution)/shard_map/ppermute | solution.py:26
  67.1 6.5 %collective-permute-start.6 = (bf16[32,128,128]{2,1,0:T(8,128)(2,1)}, bf16[32,128,128]{2,1,0:T(8,128)(2,1)}, u32[]{:S(2)}, u32[]{:S(2)}) collective-permute-start(bf16[32,128,128]{2,1,0:T(8,128)(2,1)} %collective-permute-done.1.refs_6_), channel_id=1, source_target_pairs={{0,1},{1,0},{2,3},{3,2},{4,5},{5,4},{6,7},{7,6},{8,9},{9,8},{10,11... | collective-permute-start | bytes 3145736 | tf_op jit(solution)/shard_map/ppermute | solution.py:26
  67.1 6.5 %collective-permute-start.5 = (bf16[32,128,128]{2,1,0:T(8,128)(2,1)S(1)}, bf16[32,128,128]{2,1,0:T(8,128)(2,1)}, u32[]{:S(2)}, u32[]{:S(2)}) collective-permute-start(bf16[32,128,128]{2,1,0:T(8,128)(2,1)S(1)} %collective-permute-done.refs_4_), channel_id=1, source_target_pairs={{0,1},{1,0},{2,3},{3,2},{4,5},{5,4},{6,7},{7,6},{8,9},{9,8},{10,11... | collective-permute-start | bytes 3145736 | tf_op jit(solution)/shard_map/ppermute | solution.py:26
  67.6 24.7 %collective-permute-start.3 = (bf16[32,128,128]{2,1,0:T(8,128)(2,1)S(1)}, bf16[32,128,128]{2,1,0:T(8,128)(2,1)}, u32[]{:S(2)}, u32[]{:S(2)}) collective-permute-start(bf16[32,128,128]{2,1,0:T(8,128)(2,1)S(1)} %collective-permute-done.refs_4_), channel_id=1, source_target_pairs={{0,3},{1,6},{2,5},{3,0},{4,7},{5,2},{6,1},{7,4},{8,11},{9,14},{10,... | collective-permute-start | bytes 3145736 | tf_op jit(solution)/shard_map/ppermute | solution.py:439
  68.8 25.9 %collective-permute-start.2 = (bf16[32,128,128]{2,1,0:T(8,128)(2,1)S(1)}, bf16[32,128,128]{2,1,0:T(8,128)(2,1)}, u32[]{:S(2)}, u32[]{:S(2)}) collective-permute-start(bf16[32,128,128]{2,1,0:T(8,128)(2,1)S(1)} %collective-permute-done.refs_4_), channel_id=1, source_target_pairs={{0,2},{1,7},{2,4},{3,1},{4,6},{5,3},{6,0},{7,5},{8,10},{9,15},{10,... | collective-permute-start | bytes 3145736 | tf_op jit(solution)/shard_map/ppermute | solution.py:438
  94.7 34.0 %copy-start.1 = (f32[4,4,128,128]{3,2,1,0:T(8,128)S(1)}, f32[4,4,128,128]{3,2,1,0:T(8,128)}, u32[]{:S(2)}) copy-start(f32[4,4,128,128]{3,2,1,0:T(8,128)} %get-tuple-element.32.before_ref) | copy-start | bytes 3145732
  94.7 34.0 %copy-start.2 = (bf16[512,512]{1,0:T(8,128)(2,1)S(1)}, bf16[512,512]{1,0:T(8,128)(2,1)}, u32[]{:S(2)}) copy-start(bf16[512,512]{1,0:T(8,128)(2,1)} %get-tuple-element.31.decayed_ref) | copy-start | bytes 1572868
  102.4 26.3 %copy-start = (f32[512,512]{1,0:T(8,128)S(1)}, f32[512,512]{1,0:T(8,128)}, u32[]{:S(2)}) copy-start(f32[512,512]{1,0:T(8,128)} %get-tuple-element.30.inner_ref) | copy-start | bytes 3145732
  102.4 26.3 %copy-start.3 = (f32[16,128]{1,0:T(8,128)S(1)}, f32[16,128]{1,0:T(8,128)}, u32[]{:S(2)}) copy-start(f32[16,128]{1,0:T(8,128)} %get-tuple-element.33.fade_ref) | copy-start | bytes 24580
